TPU v7x, 256 devices: a whole 4x4x8 slice. The times are simulated.
256 devices in a mesh: ctx: 32 (over x, z), head: 8 (over y, core).
Axes of the slice: x: 4, y: 4, z: 8, core: 2. Of those that a mesh axis runs over, the one named last changes fastest.
Arguments:
- query: bfloat16 [6144, 73728], P('ctx', 'head'), may hold values from -40 to 40
- latent: bfloat16 [6144, 576], P('ctx'), may hold values from -6 to 6
- segment: int32 [6144], P('ctx'), may hold values from 0 to 63, never falling along the last dimension, each value on 1 to 385 neighbouring positions
- d_out: bfloat16 [6144, 65536], P('ctx', 'head'), may hold values from -6 to 6
Outputs:
- attended: bfloat16 [6144, 65536], P('ctx', 'head')
- d_query: bfloat16 [6144, 73728], P('ctx', 'head')
- d_latent: float32 [6144, 576], P('ctx')
Inputs may be any that keep to these rules, and one draw needn't show every extreme that they name: `segment`: document ids never fall along the window; every document has 1 to 385 tokens and one has exactly 385.
All inputs are finite; a program needn't handle non-finite values.
Results may differ from a plain program's by a relative error of at most 0.017.
Values may be sent and summed in bfloat16 or wider, within the bound.
A program may use at most 128 MiB of HBM per device.

v0:
```python
import jax
import jax.numpy as jnp
from jax import lax
from jax.sharding import PartitionSpec as P

SPAN = 2


score_scale = 192.0 ** (-0.5)


def shifted(value, axis, by):
    devices = lax.axis_size(axis)
    pairs = [(i, i + by) for i in range(devices) if 0 <= i + by < devices]
    return lax.ppermute(value, axis, pairs)


def body(query, latent, segment, d_out):
    rows = latent.shape[0]
    width = latent.shape[1]
    heads = query.shape[1] // width
    latent_w = d_out.shape[1] // heads
    here = lax.axis_index("ctx")
    received = []
    for back in range(1, SPAN + 1):
        received.append(shifted((latent, segment), "ctx", back))
    key_parts = []
    seg_parts = []
    for back in range(SPAN, 0, -1):
        block, seg_block = received[back - 1]
        key_parts.append(block)
        seg_parts.append(jnp.where(here >= back, seg_block, -1))
    keys = jnp.concatenate(key_parts + [latent], 0)
    seg_keys = jnp.concatenate(seg_parts + [segment], 0)
    queries = query.reshape(rows, heads, width)
    grads = d_out.reshape(rows, heads, latent_w)
    qpos = jnp.arange(rows, dtype=jnp.int32) + SPAN * rows
    kpos = jnp.arange(keys.shape[0], dtype=jnp.int32)
    allowed = (segment[:, None] == seg_keys[None, :]) & (kpos[None, :] <= qpos[:, None])
    scores = (
        jnp.einsum("qhd,kd->hqk", queries, keys, preferred_element_type=jnp.float32) * score_scale
    )
    scores = jnp.where(allowed[None], scores, -1e30)
    top = jnp.max(scores, -1, keepdims=True)
    expo = jnp.where(allowed[None], jnp.exp(scores - top), 0.0)
    prob = expo / jnp.sum(expo, -1, keepdims=True)
    prob_low = prob.astype(jnp.bfloat16)
    values = keys[:, :latent_w]
    attended = jnp.einsum(
        "hqk,kd->qhd", prob_low, values, preferred_element_type=jnp.float32
    ).astype(jnp.bfloat16)
    d_prob = jnp.einsum("qhd,kd->hqk", grads, values, preferred_element_type=jnp.float32)
    delta = jnp.einsum("qhd,qhd->hq", grads, attended, preferred_element_type=jnp.float32)
    d_score = (score_scale * prob * (d_prob - delta[:, :, None])).astype(jnp.bfloat16)
    d_query = jnp.einsum("hqk,kd->qhd", d_score, keys, preferred_element_type=jnp.float32).astype(
        jnp.bfloat16
    )
    d_keys = jnp.einsum("hqk,qhd->kd", d_score, queries, preferred_element_type=jnp.float32)
    d_vals = jnp.einsum("hqk,qhd->kd", prob_low, grads, preferred_element_type=jnp.float32)
    d_keys = d_keys + jnp.pad(d_vals, ((0, 0), (0, width - latent_w)))
    stacked = d_keys.reshape(SPAN + 1, rows, width)
    total = stacked[SPAN]
    for back in range(1, SPAN + 1):
        total = total + shifted(stacked[SPAN - back].astype(jnp.bfloat16), "ctx", -back).astype(
            jnp.float32
        )
    d_latent = lax.psum(total, "head")
    return (
        attended.reshape(rows, heads * latent_w),
        d_query.reshape(rows, heads * width),
        d_latent,
    )


def solution(mesh):
    in_specs = (P("ctx", "head"), P("ctx", None), P("ctx"), P("ctx", "head"))
    out_specs = (P("ctx", "head"), P("ctx", "head"), P("ctx", None))
    return jax.shard_map(body, mesh=mesh, in_specs=in_specs, out_specs=out_specs, check_vma=False)
```

profile of v0, /device:TPU:7, one launch (start us, length us, event | category | flops | bytes accessed | tf_op | source)
XLA Modules:
  0.0 167.7 jit_solution(8418870780687852021)
XLA Ops:
  7.2 5.2 %collective-permute-start = (bf16[192,576]{1,0:T(8,128)(2,1)}, bf16[192,576]{1,0:T(8,128)(2,1)}, u32[]{:S(2)}, u32[]{:S(2)}) collective-permute-start(bf16[192,576]{1,0:T(8,128)(2,1)} %param.5), channel_id=1, source_target_pairs={{0,16},{8,24},{16,32},{24,40},{32,48},{40,56},{48,64},{56,72},{64,... | collective-permute-start | bytes 663560 | tf_op jit(solution)/shard_map/ppermute | solution.py:15
  12.4 3.5 %collective-permute-start.1 = (bf16[192,576]{1,0:T(8,128)(2,1)}, bf16[192,576]{1,0:T(8,128)(2,1)}, u32[]{:S(2)}, u32[]{:S(2)}) collective-permute-start(bf16[192,576]{1,0:T(8,128)(2,1)} %param.5), channel_id=1, source_target_pairs={{0,8},{8,16},{16,24},{24,32},{32,40},{40,48},{48,56},{56,64},{64,7... | collective-permute-start | bytes 663560 | tf_op jit(solution)/shard_map/ppermute | solution.py:15
  16.0 4.8 %collective-permute-start.3 = (s32[192]{0:T(256)}, s32[192]{0:T(256)S(1)}, u32[]{:S(2)}, u32[]{:S(2)}) collective-permute-start(s32[192]{0:T(256)} %param.6), channel_id=1, source_target_pairs={{0,8},{8,16},{16,24},{24,32},{32,40},{40,48},{48,56},{56,64},{64,7... | collective-permute-start | bytes 2312 | tf_op jit(solution)/shard_map/ppermute | solution.py:15
  20.7 3.1 %collective-permute-start.2 = (s32[192]{0:T(256)}, s32[192]{0:T(256)S(1)}, u32[]{:S(2)}, u32[]{:S(2)}) collective-permute-start(s32[192]{0:T(256)} %param.6), channel_id=1, source_target_pairs={{0,16},{8,24},{16,32},{24,40},{32,48},{40,56},{48,64},{56,72},{64,... | collective-permute-start | bytes 2312 | tf_op jit(solution)/shard_map/ppermute | solution.py:15
  23.8 7.0 %reshape.79 = bf16[192,16,576]{2,1,0:T(8,128)(2,1)} reshape(bf16[192,9216]{1,0:T(8,128)(2,1)} %param.4) | data formatting | bytes 7077888 | tf_op jit(solution)/shard_map/reshape | solution.py:35
  30.8 1.3 copy.26
  34.6 5.8 %fusion.9 = f32[576,192,16]{0,1,2:T(8,128)} fusion(bf16[192,16,576]{2,1,0:T(8,128)(2,1)S(1)} %copy-done.3, bf16[576,576]{1,0:T(8,128)(2,1)S(1)} %constant_dynamic-update-slice_fusion), kind=kOutput, calls=%fused_computation.15 | convolution fusion | flops 2038431744 | bytes 11280384 | tf_op jit(solution)/shard_map/qhd,kd->hqk/dot_general | solution.py:41
  40.4 9.9 %fusion.32 = (f32[16,192]{1,0:T(8,128)S(1)}, f32[16,192,576]{2,1,0:T(8,128)S(1)}) fusion(f32[576,192,16]{0,1,2:T(8,128)} %fusion.9, pred[192,576]{1,0:T(8,128)(4,1)S(1)} %fusion.28), kind=kOutput, calls=%fused_computation.45 | output fusion | flops 12386879 | bytes 14278656 | tf_op jit(solution)/shard_map/sub | solution.py:45
  51.2 2.1 %copy-done.1 = f32[16,192,576]{2,1,0:T(8,128)} copy-done((f32[16,192,576]{2,1,0:T(8,128)}, f32[16,192,576]{2,1,0:T(8,128)S(1)}, u32[]{:S(2)}) %copy-start.1) | copy-done | bytes 7077912
  53.3 2.6 %bitcast_convert_fusion = (f32[16,192,512]{2,1,0:T(8,128)S(1)}, bf16[512,16,192]{0,2,1:T(8,128)(2,1)S(1)}) fusion(bf16[16,192,576]{2,1,0:T(8,128)(2,1)S(1)} %fusion.11, bf16[576,576]{1,0:T(8,128)(2,1)S(1)} %constant_dynamic-update-slice_fusion), kind=kOutput, calls=%fused_computation.22 | convolution fusion | flops 1815085056 | bytes 13959168 | tf_op jit(solution)/shard_map/hqk,kd->qhd/dot_general | solution.py:49
  56.0 3.8 %multiply_reduce_fusion = f32[16,192]{0,1:T(8,128)S(1)} fusion(f32[16,192,512]{2,1,0:T(8,128)S(1)} %get-tuple-element.7, bf16[192,16,512]{2,1,0:T(8,128)(2,1)S(1)} %bitcast.59), kind=kLoop, calls=%fused_computation.6 | loop fusion | flops 4715520 | bytes 9449472
  59.9 5.2 %fusion.22 = f32[576,512]{1,0:T(8,128)S(1)} fusion(bf16[16,192,576]{2,1,0:T(8,128)(2,1)} %copy-done, bf16[24,16,8,512]{3,2,1,0:T(8,128)(2,1)} %bitcast.60), kind=kOutput, calls=%fused_computation.27 | convolution fusion | flops 1811939328 | bytes 7864320 | tf_op jit(solution)/shard_map/hqk,qhd->kd/dot_general | solution.py:59
  65.3 4.8 %fusion.2 = bf16[16,192,576]{2,1,0:T(8,128)(2,1)S(1)} fusion(f32[16,192]{1,0:T(8,128)S(1)} %copy.23, f32[16,192,576]{2,1,0:T(8,128)S(1)} %copy-done.2, f32[16,192]{1,0:T(8,128)S(1)} %get-tuple-element.5, bf16[24,16,8,512]{3,2,1,0:T(8,128)(2,1)} %bitcast.61, bf16[576,576]{1,0:T(8,128)(2,1)S(1)} %copy-done.7), kind=kOutput, calls=%fused_computation.3 | convolution fusion | flops 1820786688 | bytes 15171584 | tf_op jit(solution)/shard_map/qhd,kd->hqk/dot_general | solution.py:52
  70.2 3.1 %fusion.33 = (bf16[576,576]{1,0:T(8,128)(2,1)S(1)}, f32[576,576]{1,0:T(8,128)S(1)}) fusion(f32[576,512]{1,0:T(8,128)S(1)} %fusion.22, bf16[16,192,576]{2,1,0:T(8,128)(2,1)S(1)} %fusion.2, bf16[192,16,576]{2,1,0:T(8,128)(2,1)S(1)} %copy-done.4), kind=kOutput, calls=%fused_computation.46 | convolution fusion | flops 2039095296 | bytes 10248192 | tf_op jit(solution)/shard_map/hqk,qhd->kd/dot_general | solution.py:58
  73.4 5.2 %collective-permute-start.5 = (bf16[192,576]{1,0:T(8,128)(2,1)S(1)}, bf16[192,576]{1,0:T(8,128)(2,1)S(1)}, u32[]{:S(2)}, u32[]{:S(2)}) collective-permute-start(bf16[192,576]{1,0:T(8,128)(2,1)S(1)} %get-tuple-element.4), channel_id=1, source_target_pairs={{16,0},{24,8},{32,16},{40,24},{48,32},{56,40},{64,48},{72,56},{80,... | collective-permute-start | bytes 663560 | tf_op jit(solution)/shard_map/ppermute | solution.py:15
  78.6 2.9 %collective-permute-start.4 = (bf16[192,576]{1,0:T(8,128)(2,1)S(1)}, bf16[192,576]{1,0:T(8,128)(2,1)S(1)}, u32[]{:S(2)}, u32[]{:S(2)}) collective-permute-start(bf16[192,576]{1,0:T(8,128)(2,1)S(1)} %get-tuple-element.3), channel_id=1, source_target_pairs={{8,0},{16,8},{24,16},{32,24},{40,32},{48,40},{56,48},{64,56},{72,6... | collective-permute-start | bytes 663560 | tf_op jit(solution)/shard_map/ppermute | solution.py:15
  81.5 6.0 %collective-permute-done.5 = bf16[192,576]{1,0:T(8,128)(2,1)S(1)} collective-permute-done((bf16[192,576]{1,0:T(8,128)(2,1)S(1)}, bf16[192,576]{1,0:T(8,128)(2,1)S(1)}, u32[]{:S(2)}, u32[]{:S(2)}) %collective-permute-start.5) | collective-permute-done | bytes 221216 | tf_op jit(solution)/shard_map/ppermute | solution.py:15
  87.5 7.1 %collective-permute-done.4 = bf16[192,576]{1,0:T(8,128)(2,1)S(1)} collective-permute-done((bf16[192,576]{1,0:T(8,128)(2,1)S(1)}, bf16[192,576]{1,0:T(8,128)(2,1)S(1)}, u32[]{:S(2)}, u32[]{:S(2)}) %collective-permute-start.4) | collective-permute-done | bytes 221216 | tf_op jit(solution)/shard_map/ppermute | solution.py:15
  95.5 6.0 %convert_bitcast_fusion = bf16[192,16,576]{2,0,1:T(8,128)(2,1)S(1)} fusion(bf16[16,192,576]{2,1,0:T(8,128)(2,1)} %copy-done.10, bf16[576,576]{1,0:T(8,128)(2,1)} %copy-done.6), kind=kOutput, calls=%fused_computation.8 | convolution fusion | flops 2040201216 | bytes 7741440 | tf_op jit(solution)/shard_map/hqk,kd->qhd/dot_general | solution.py:55
  101.5 2.1 %copy.25 = bf16[16,24,8,512]{3,2,0,1:T(8,128)(2,1)} copy(bf16[16,24,8,512]{3,2,1,0:T(8,128)(2,1)S(1)} %bitcast.58) | data formatting | bytes 6291456 | tf_op jit(solution)/shard_map/reshape | solution.py:69
  103.5 4.1 %copy.14 = bf16[192,16,576]{2,1,0:T(8,128)(2,1)} copy(bf16[192,16,576]{2,0,1:T(8,128)(2,1)S(1)} %convert_bitcast_fusion) | data formatting | bytes 7077888 | tf_op jit(solution)/shard_map/convert_element_type | solution.py:55
  107.7 7.0 %reshape.82 = bf16[192,9216]{1,0:T(8,128)(2,1)} reshape(bf16[192,16,576]{2,1,0:T(8,128)(2,1)} %copy.14) | data formatting | bytes 7077888 | tf_op jit(solution)/shard_map/reshape | solution.py:70
  114.7 44.3 %all-reduce.3.cloned.1.call-done = f32[192,576]{1,0:T(8,128)} async-done(((f32[192,576]{1,0:T(8,128)}), f32[192,576]{1,0:T(8,128)}) %all-reduce.3.cloned.1.call-update) | async-done | bytes 442384 | tf_op jit(solution)/shard_map/psum | solution.py:67
  159.1 1.8 %copy.51 = f32[192,576]{1,0:T(8,128)} copy(f32[192,576]{1,0:T(8,128)} %all-reduce.3.cloned.1.call-done) | data formatting | bytes 884736
  (39 shorter events, 4.5 us)
Async XLA Ops:
  7.2 23.7 %copy-start.5 = (bf16[192,8192]{1,0:T(8,128)(2,1)S(1)}, bf16[192,8192]{1,0:T(8,128)(2,1)}, u32[]{:S(2)}) copy-start(bf16[192,8192]{1,0:T(8,128)(2,1)} %param.7) | copy-start | bytes 9437188
  7.2 151.9 %all-reduce.3.cloned.1.call-start = ((), (), s32[]{:S(2)}) async-start(), calls=%async_computation | async-start | bytes 983040 | tf_op jit(solution)/shard_map/psum | solution.py:67
  7.2 25.3 %collective-permute-start = (bf16[192,576]{1,0:T(8,128)(2,1)}, bf16[192,576]{1,0:T(8,128)(2,1)}, u32[]{:S(2)}, u32[]{:S(2)}) collective-permute-start(bf16[192,576]{1,0:T(8,128)(2,1)} %param.5), channel_id=1, source_target_pairs={{0,16},{8,24},{16,32},{24,40},{32,48},{40,56},{48,64},{56,72},{64,... | collective-permute-start | bytes 663560 | tf_op jit(solution)/shard_map/ppermute | solution.py:15
  12.4 21.1 %collective-permute-start.1 = (bf16[192,576]{1,0:T(8,128)(2,1)}, bf16[192,576]{1,0:T(8,128)(2,1)}, u32[]{:S(2)}, u32[]{:S(2)}) collective-permute-start(bf16[192,576]{1,0:T(8,128)(2,1)} %param.5), channel_id=1, source_target_pairs={{0,8},{8,16},{16,24},{24,32},{32,40},{40,48},{48,56},{56,64},{64,7... | collective-permute-start | bytes 663560 | tf_op jit(solution)/shard_map/ppermute | solution.py:15
  16.0 16.2 %collective-permute-start.3 = (s32[192]{0:T(256)}, s32[192]{0:T(256)S(1)}, u32[]{:S(2)}, u32[]{:S(2)}) collective-permute-start(s32[192]{0:T(256)} %param.6), channel_id=1, source_target_pairs={{0,8},{8,16},{16,24},{24,32},{32,40},{40,48},{48,56},{56,64},{64,7... | collective-permute-start | bytes 2312 | tf_op jit(solution)/shard_map/ppermute | solution.py:15
  20.7 11.5 %collective-permute-start.2 = (s32[192]{0:T(256)}, s32[192]{0:T(256)S(1)}, u32[]{:S(2)}, u32[]{:S(2)}) collective-permute-start(s32[192]{0:T(256)} %param.6), channel_id=1, source_target_pairs={{0,16},{8,24},{16,32},{24,40},{32,48},{40,56},{48,64},{56,72},{64,... | collective-permute-start | bytes 2312 | tf_op jit(solution)/shard_map/ppermute | solution.py:15
  30.8 1.4 copy-start.9
  30.8 3.7 %copy-start.8 = (bf16[192,576]{1,0:T(8,128)(2,1)S(1)}, bf16[192,576]{1,0:T(8,128)(2,1)}, u32[]{:S(2)}) copy-start(bf16[192,576]{1,0:T(8,128)(2,1)} %param.5) | copy-start | bytes 663556
  30.8 3.7 %copy-start.3 = (bf16[192,16,576]{2,1,0:T(8,128)(2,1)S(1)}, bf16[192,16,576]{2,1,0:T(8,128)(2,1)}, u32[]{:S(2)}) copy-start(bf16[192,16,576]{2,1,0:T(8,128)(2,1)} %reshape.79) | copy-start | bytes 10616836
  34.6 16.7 %copy-start.6 = (bf16[576,576]{1,0:T(8,128)(2,1)}, bf16[576,576]{1,0:T(8,128)(2,1)S(1)}, u32[]{:S(2)}) copy-start(bf16[576,576]{1,0:T(8,128)(2,1)S(1)} %constant_dynamic-update-slice_fusion) | copy-start | bytes 1990660
  50.3 3.1 %copy-start.1 = (f32[16,192,576]{2,1,0:T(8,128)}, f32[16,192,576]{2,1,0:T(8,128)S(1)}, u32[]{:S(2)}) copy-start(f32[16,192,576]{2,1,0:T(8,128)S(1)} %get-tuple-element.6) | copy-start | bytes 21233668
  53.3 2.6 %copy-start = (bf16[16,192,576]{2,1,0:T(8,128)(2,1)}, bf16[16,192,576]{2,1,0:T(8,128)(2,1)S(1)}, u32[]{:S(2)}) copy-start(bf16[16,192,576]{2,1,0:T(8,128)(2,1)S(1)} %fusion.11) | copy-start | bytes 10616836
  59.9 5.3 %copy-start.2 = (f32[16,192,576]{2,1,0:T(8,128)S(1)}, f32[16,192,576]{2,1,0:T(8,128)}, u32[]{:S(2)}) copy-start(f32[16,192,576]{2,1,0:T(8,128)} %copy-done.1) | copy-start | bytes 21233668
  59.9 5.4 %copy-start.7 = (bf16[576,576]{1,0:T(8,128)(2,1)S(1)}, bf16[576,576]{1,0:T(8,128)(2,1)}, u32[]{:S(2)}) copy-start(bf16[576,576]{1,0:T(8,128)(2,1)} %copy-done.6) | copy-start | bytes 1990660
  65.3 4.8 %copy-start.4 = (bf16[192,16,576]{2,1,0:T(8,128)(2,1)S(1)}, bf16[192,16,576]{2,1,0:T(8,128)(2,1)}, u32[]{:S(2)}) copy-start(bf16[192,16,576]{2,1,0:T(8,128)(2,1)} %reshape.79) | copy-start | bytes 10616836
  70.2 3.1 %copy-start.10 = (bf16[16,192,576]{2,1,0:T(8,128)(2,1)}, bf16[16,192,576]{2,1,0:T(8,128)(2,1)S(1)}, u32[]{:S(2)}) copy-start(bf16[16,192,576]{2,1,0:T(8,128)(2,1)S(1)} %fusion.2) | copy-start | bytes 10616836
  73.4 14.1 %collective-permute-start.5 = (bf16[192,576]{1,0:T(8,128)(2,1)S(1)}, bf16[192,576]{1,0:T(8,128)(2,1)S(1)}, u32[]{:S(2)}, u32[]{:S(2)}) collective-permute-start(bf16[192,576]{1,0:T(8,128)(2,1)S(1)} %get-tuple-element.4), channel_id=1, source_target_pairs={{16,0},{24,8},{32,16},{40,24},{48,32},{56,40},{64,48},{72,56},{80,... | collective-permute-start | bytes 663560 | tf_op jit(solution)/shard_map/ppermute | solution.py:15
  78.6 16.0 %collective-permute-start.4 = (bf16[192,576]{1,0:T(8,128)(2,1)S(1)}, bf16[192,576]{1,0:T(8,128)(2,1)S(1)}, u32[]{:S(2)}, u32[]{:S(2)}) collective-permute-start(bf16[192,576]{1,0:T(8,128)(2,1)S(1)} %get-tuple-element.3), channel_id=1, source_target_pairs={{8,0},{16,8},{24,16},{32,24},{40,32},{48,40},{56,48},{64,56},{72,6... | collective-permute-start | bytes 663560 | tf_op jit(solution)/shard_map/ppermute | solution.py:15
Sparse Core Ops, SparseCore 0:
  95.6 63.3 all-reduce.2
where the time goes:
time: 171 us; the launch traced here: 168 us
  waiting for transfers between devices  57.5 us (34%)
  local copies, waits for them, and re-layouts  27.9 us (16%)
  matrix products  27.6 us (16%)
  starting transfers between devices  24.7 us (14%)
  other arithmetic  15.8 us (9%)
  between operations  14.3 us (8%)
    psum x1, waiting for transfers between devices, body(): d_latent = lax.psum(total, 'head')  44.3 us
    ppermute x6, starting transfers between devices, shifted(): return lax.ppermute(value, axis, pairs)  24.6 us
    ppermute x6, waiting for transfers between devices, shifted(): return lax.ppermute(value, axis, pairs)  13.2 us
    sub x1, other arithmetic, body(): expo = jnp.where(allowed[None], jnp.exp(scores - top), 0.0)  9.9 us
    unnamed x26, local copies, waits for them, and re-layouts  7.48 us
    reshape x1, local copies, waits for them, and re-layouts, body(): d_query.reshape(rows, heads * width)  7.05 us
    reshape x1, local copies, waits for them, and re-layouts, body(): queries = query.reshape(rows, heads, width)  6.98 us
    dot_general x1, matrix products, body(): jnp.einsum('hqk,kd->qhd', d_score, keys, preferred_element_type=jnp.float32)  5.98 us
  transfers between devices with their start and end apart: 7, of which 3 were waited for; matrix products, arithmetic and copies ran while one was open for 17% of the time, Pallas kernels for 0%

commit v1 on v0

v1 whole, which is shorter than its diff:
```python
import jax
import jax.numpy as jnp
from jax import lax
from jax.experimental import pallas as pl
from jax.experimental.pallas import tpu as pltpu
from jax.sharding import PartitionSpec as P

SPAN = 2
TOK = 192
HEADS = 16
PAIRS = HEADS // 2
LAT = 512
WIDTH = 576
PADW = 640
WIN = 512
NCTX = 32
SLICE = 48
HALF = 24
SCALE = 192.0 ** -0.5
SCALE2 = SCALE * 1.4426950408889634
bf16 = jnp.bfloat16
f32 = jnp.float32

GROUPS = ((0, 0, 128, 2, 4, 0), (64, 128, 64, 4, 2, 8))


def dot(a, b):
    return jnp.dot(a, b, preferred_element_type=f32)


def remote(src, dst, send, recv, ctx, head):
    return pltpu.make_async_remote_copy(
        src_ref=src,
        dst_ref=dst,
        send_sem=send,
        recv_sem=recv,
        device_id={"ctx": ctx, "head": head},
        device_id_type=pl.DeviceIdType.MESH,
    )


def kernel(
    q_hbm, lat_ref, seg_ref, do_hbm,
    att_hbm, dq_hbm, dl_hbm,
    q, do, ke, ko, kte, kto, pst, dst, p, ds, att, dq, bias0, bias1, segs,
    acce, acco, accv, hsum, xs_send, xs_recv, yb_send, yb_recv, zb_send, zb_recv,
    ob_send, ob_recv, tsum, fx_recv, out_v,
    in_sem, out_sem, send_sem, recv_sem,
):
    here = lax.axis_index("ctx")
    head = lax.axis_index("head")
    y = head // 2
    c = lax.rem(head, 2)
    sib = y * 2 + 1 - c

    def peer(d):
        return lax.rem(y + d, 4) * 2 + c

    nxt = lax.rem(here + 1 + c, NCTX)
    prv = lax.rem(here + NCTX - 1 - c, NCTX)

    loads = []
    for i in range(PAIRS):
        loads.append(
            (
                pltpu.make_async_copy(
                    q_hbm.at[:, pl.ds(2 * WIDTH * i, 2 * WIDTH)], q.at[i], in_sem.at[0, i]
                ),
                pltpu.make_async_copy(
                    do_hbm.at[:, pl.ds(2 * LAT * i, 2 * LAT)], do.at[i], in_sem.at[1, i]
                ),
            )
        )
    for pair in loads:
        for cp in pair:
            cp.start()

    barrier = pltpu.get_barrier_semaphore()
    for ctx, hd in ((nxt, head), (prv, head), (here, sib), (here, peer(1)), (here, peer(2)), (here, peer(3))):
        pl.semaphore_signal(
            barrier, inc=1, device_id={"ctx": ctx, "head": hd}, device_id_type=pl.DeviceIdType.MESH
        )
    own = lat_ref[...]
    zcol = jnp.zeros((TOK, PADW - WIDTH), bf16)
    ke[2 * TOK :, :] = jnp.concatenate([own, zcol], 1)
    segs[2] = seg_ref[...]
    pl.semaphore_wait(barrier, 6)

    mine = (1 - c) * TOK
    other = c * TOK

    def rows(base, yy):
        return pl.ds(pl.multiple_of(base + yy * SLICE, 16), SLICE)

    h1 = remote(
        ke.at[rows(2 * TOK, y)], ke.at[rows(mine, y)], send_sem.at[0], recv_sem.at[0], nxt, head
    )
    h1.start()
    s1 = remote(segs.at[2], segs.at[1 - c], send_sem.at[1], recv_sem.at[1], nxt, head)
    s1.start()
    s1.wait_recv()
    s2 = remote(segs.at[1 - c], segs.at[1 - c], send_sem.at[2], recv_sem.at[2], here, sib)
    s2.start()
    h1.wait_recv()
    sends = [h1, s1, s2]
    h2 = []
    for d in (1, 3, 2):
        cp = remote(
            ke.at[rows(mine, y)], ke.at[rows(mine, y)],
            send_sem.at[2 + d], recv_sem.at[2 + d], here, peer(d),
        )
        cp.start()
        h2.append((d, cp))
    sends += [cp for _, cp in h2]
    fwd = [
        remote(
            ke.at[rows(mine, y)], ke.at[rows(mine, y)], send_sem.at[6], recv_sem.at[6], here, sib
        )
    ]
    fwd[0].start()
    for d, cp in h2:
        cp.wait_recv()
        yy = lax.rem(y + 4 - d, 4)
        fw = remote(
            ke.at[rows(mine, yy)], ke.at[rows(mine, yy)],
            send_sem.at[6 + d], recv_sem.at[6 + d], here, sib,
        )
        fw.start()
        fwd.append(fw)
    s2.wait_recv()
    sends += fwd

    seg_row = jnp.concatenate(
        [
            jnp.where(here >= 2, segs[0], -1),
            jnp.where(here >= 1, segs[1], -1),
            segs[2],
        ],
        1,
    )
    seg_keys = jnp.broadcast_to(seg_row, (TOK, 3 * TOK))
    tok = lax.broadcasted_iota(jnp.int32, (TOK, 3 * TOK), 0) + 2 * TOK
    key = lax.broadcasted_iota(jnp.int32, (TOK, 3 * TOK), 1)
    seg_q = jnp.sum(jnp.where(tok == key, seg_keys, 0), 1, keepdims=True)
    bias = jnp.where((seg_q == seg_keys) & (key <= tok), 0.0, -1e30)
    bias0[...] = bias[:128, :WIN]
    bias1[...] = bias[128:, 64:]

    for fw in fwd:
        fw.wait_recv()
    for cp in sends:
        cp.wait_send()

    kev = ke[...]
    zk = jnp.zeros((3 * TOK, PADW - WIDTH), bf16)
    ko[...] = jnp.concatenate([zk, kev[:, :WIDTH]], 1)
    for g in (0, 1):
        st = GROUPS[g][0]
        kt = kev[st : st + WIN].T
        kte[g] = kt
        kto[g] = jnp.concatenate([jnp.zeros((PADW - WIDTH, WIN), bf16), kt[:WIDTH]], 0)

    def qrows(g, i, par):
        _, t0, toks, n, _, _ = GROUPS[g]
        return q[pl.ds(i * n, n), t0 : t0 + toks, par * LAT : par * LAT + PADW].reshape(256, PADW)

    def dorows(g, i, par):
        _, t0, toks, n, _, _ = GROUPS[g]
        return do[pl.ds(i * n, n), t0 : t0 + toks, par * LAT : par * LAT + LAT].reshape(256, LAT)

    def attend(g, i, par):
        _, _, toks, n, _, first = GROUPS[g]
        bias_ref = (bias0, bias1)[g]
        s = dot(qrows(g, i, par), (kte, kto)[par][g])
        dp = dot(dorows(g, i, par), kte[g, :LAT, :])
        t = ((s * SCALE2).reshape(n, toks, WIN) + bias_ref[...][None]).reshape(256, WIN)
        e = jnp.exp2(t - jnp.max(t, 1, keepdims=True))
        pr = e * (1.0 / jnp.sum(e, 1, keepdims=True))
        delta = jnp.sum(pr * dp, 1, keepdims=True)
        d = (pr * (dp - delta) * SCALE).astype(bf16)
        pr = pr.astype(bf16)
        j = first + i * 2 + par
        p[j] = pr
        ds[j] = d
        pst[j] = pr.T
        dst[j] = d.T

    def wait_pair(i):
        pltpu.make_async_copy(
            q_hbm.at[:, pl.ds(0, 2 * WIDTH)], q.at[i], in_sem.at[0, i]
        ).wait()
        pltpu.make_async_copy(
            do_hbm.at[:, pl.ds(0, 2 * LAT)], do.at[i], in_sem.at[1, i]
        ).wait()

    def step0(i, _):
        wait_pair(2 * i)
        wait_pair(2 * i + 1)
        attend(0, i, 0)
        attend(0, i, 1)
        return 0

    def step1(i, _):
        attend(1, i, 0)
        attend(1, i, 1)
        return 0

    lax.fori_loop(0, 4, step0, 0)
    lax.fori_loop(0, 2, step1, 0)

    acce[...] = jnp.zeros_like(acce)
    acco[...] = jnp.zeros_like(acco)
    accv[...] = jnp.zeros_like(accv)

    def key_grads(lo, hi):
        for g in (0, 1):
            st, _, _, _, count, first = GROUPS[g]
            a, b = max(lo, st), min(hi, st + WIN)

            def step(i, _):
                j = first + 2 * i
                w = slice(a - st, b - st)
                acce[a:b] += dot(dst[j, w], qrows(g, i, 0))
                acco[a:b] += dot(dst[j + 1, w], qrows(g, i, 1))
                accv[a:b] += dot(pst[j, w], dorows(g, i, 0)) + dot(pst[j + 1, w], dorows(g, i, 1))
                return 0

            lax.fori_loop(0, count, step, 0)
        tot = acce[lo:hi, :WIDTH] + acco[lo:hi, PADW - WIDTH :]
        hsum[lo:hi, :LAT] = tot[:, :LAT] + accv[lo:hi]
        hsum[lo:hi, LAT:] = tot[:, LAT:]

    key_grads(0, 2 * TOK)
    xs_send[...] = hsum[pl.ds(pl.multiple_of(other, 16), TOK)].astype(bf16)
    r1 = remote(xs_send, xs_recv, send_sem.at[10], recv_sem.at[10], here, sib)
    r1.start()
    key_grads(2 * TOK, 3 * TOK)

    ob_send[...] = hsum[2 * TOK :].astype(bf16)
    r1.wait_recv()
    keep = hsum[pl.ds(pl.multiple_of(mine, 16), TOK)] + xs_recv[...].astype(f32)
    yb_send[...] = keep.astype(bf16)
    hsum[:TOK] = keep
    yb = []
    for d in (1, 3, 2):
        cp = remote(
            yb_send.at[rows(0, lax.rem(y + d, 4))], yb_recv.at[d - 1],
            send_sem.at[10 + d], recv_sem.at[10 + d], here, peer(d),
        )
        cp.start()
        yb.append(cp)
    ob = []
    for d in (1, 3, 2):
        cp = remote(
            ob_send.at[rows(0, lax.rem(y + d, 4))], ob_recv.at[d - 1],
            send_sem.at[13 + d], recv_sem.at[13 + d], here, peer(d),
        )
        cp.start()
        ob.append(cp)

    stores = []

    def outputs(g, i):
        st, t0, toks, n, _, first = GROUPS[g]
        j = first + 2 * i
        for par in (0, 1):
            o = dot(p[j + par], ke[st : st + WIN, :LAT]).astype(bf16).reshape(n, toks, LAT)
            for a in range(n):
                col = (2 * (i * n + a) + par) * LAT
                att[t0 : t0 + toks, col : col + LAT] = o[a]
        qe = dot(ds[j], ke[st : st + WIN])
        qo = dot(ds[j + 1], ko[st : st + WIN])
        full = jnp.concatenate(
            [qe[:, :LAT], qe[:, LAT:] + qo[:, : PADW - LAT], qo[:, PADW - LAT :]], 1
        )
        full = full.astype(bf16).reshape(n, toks, 2 * WIDTH)
        for a in range(n):
            col = (i * n + a) * 2 * WIDTH
            dq[t0 : t0 + toks, col : col + 2 * WIDTH] = full[a]
        at = (pl.ds(t0, toks), pl.ds(i * n * 2 * LAT, n * 2 * LAT))
        qt = (pl.ds(t0, toks), pl.ds(i * n * 2 * WIDTH, n * 2 * WIDTH))
        k = len(stores) // 2
        stores.append(pltpu.make_async_copy(att.at[at], att_hbm.at[at], out_sem.at[0, k]))
        stores.append(pltpu.make_async_copy(dq.at[qt], dq_hbm.at[qt], out_sem.at[1, k]))
        stores[-1].start()
        stores[-2].start()

    outputs(0, 0)
    outputs(0, 1)
    outputs(0, 2)
    for cp in yb:
        cp.wait_recv()
    zb_send[...] = (
        hsum[rows(0, y)]
        + yb_recv[0].astype(f32)
        + yb_recv[1].astype(f32)
        + yb_recv[2].astype(f32)
    ).astype(bf16)
    zc = remote(zb_send, zb_recv, send_sem.at[17], recv_sem.at[17], prv, head)
    zc.start()
    outputs(0, 3)
    outputs(1, 0)
    for cp in ob:
        cp.wait_recv()
    tsum[...] = (
        hsum[rows(2 * TOK, y)]
        + ob_recv[0].astype(f32)
        + ob_recv[1].astype(f32)
        + ob_recv[2].astype(f32)
    )
    outputs(1, 1)
    zc.wait_recv()
    tsum[...] += zb_recv[...].astype(f32)

    def half(cc):
        return pl.ds(pl.multiple_of(cc * HALF, 8), HALF)

    fx = remote(tsum.at[half(1 - c)], fx_recv, send_sem.at[18], recv_sem.at[18], here, sib)
    fx.start()
    fx.wait_recv()

    def place(yy, cc):
        return pl.ds(pl.multiple_of(yy * SLICE + cc * HALF, 8), HALF)

    out_v[place(y, c)] = tsum[half(c)] + fx_recv[...]
    spread = []
    for d in (1, 3, 2):
        cp = remote(
            out_v.at[place(y, c)], out_v.at[place(y, c)],
            send_sem.at[18 + d], recv_sem.at[18 + d], here, peer(d),
        )
        cp.start()
        spread.append((d, cp))
    last = [
        remote(
            out_v.at[place(y, c)], out_v.at[place(y, c)], send_sem.at[22], recv_sem.at[22], here, sib
        )
    ]
    last[0].start()
    for d, cp in spread:
        cp.wait_recv()
        yy = lax.rem(y + 4 - d, 4)
        fw = remote(
            out_v.at[place(yy, c)], out_v.at[place(yy, c)],
            send_sem.at[22 + d], recv_sem.at[22 + d], here, sib,
        )
        fw.start()
        last.append(fw)
    for cp in last:
        cp.wait_recv()
    fin = pltpu.make_async_copy(out_v, dl_hbm, out_sem.at[0, 6])
    fin.start()
    for cp in [r1, zc, fx] + yb + ob + [cp for _, cp in spread] + last:
        cp.wait_send()
    for cp in stores:
        cp.wait()
    fin.wait()


def body(query, latent, segment, d_out):
    anyspec = pl.BlockSpec(memory_space=pl.ANY)
    vspec = pl.BlockSpec(memory_space=pltpu.VMEM)
    V = pltpu.VMEM
    return pl.pallas_call(
        kernel,
        out_shape=(
            jax.ShapeDtypeStruct((TOK, HEADS * LAT), bf16),
            jax.ShapeDtypeStruct((TOK, HEADS * WIDTH), bf16),
            jax.ShapeDtypeStruct((TOK, WIDTH), f32),
        ),
        in_specs=[anyspec, vspec, vspec, anyspec],
        out_specs=(anyspec, anyspec, anyspec),
        scratch_shapes=[
            V((PAIRS, TOK, 2 * WIDTH), bf16),
            V((PAIRS, TOK, 2 * LAT), bf16),
            V((3 * TOK, PADW), bf16),
            V((3 * TOK, PADW), bf16),
            V((2, PADW, WIN), bf16),
            V((2, PADW, WIN), bf16),
            V((12, WIN, 256), bf16),
            V((12, WIN, 256), bf16),
            V((12, 256, WIN), bf16),
            V((12, 256, WIN), bf16),
            V((TOK, HEADS * LAT), bf16),
            V((TOK, HEADS * WIDTH), bf16),
            V((128, WIN), f32),
            V((64, WIN), f32),
            V((3, 1, TOK), jnp.int32),
            V((3 * TOK, PADW), f32),
            V((3 * TOK, PADW), f32),
            V((3 * TOK, LAT), f32),
            V((3 * TOK, WIDTH), f32),
            V((TOK, WIDTH), bf16),
            V((TOK, WIDTH), bf16),
            V((TOK, WIDTH), bf16),
            V((3, SLICE, WIDTH), bf16),
            V((SLICE, WIDTH), bf16),
            V((SLICE, WIDTH), bf16),
            V((TOK, WIDTH), bf16),
            V((3, SLICE, WIDTH), bf16),
            V((SLICE, WIDTH), f32),
            V((HALF, WIDTH), f32),
            V((TOK, WIDTH), f32),
            pltpu.SemaphoreType.DMA((2, PAIRS)),
            pltpu.SemaphoreType.DMA((2, PAIRS)),
            pltpu.SemaphoreType.DMA((26,)),
            pltpu.SemaphoreType.DMA((26,)),
        ],
        compiler_params=pltpu.CompilerParams(
            collective_id=0, has_side_effects=True, vmem_limit_bytes=56 << 20
        ),
    )(query, latent, segment.reshape(1, TOK), d_out)


def solution(mesh):
    in_specs = (P("ctx", "head"), P("ctx", None), P("ctx"), P("ctx", "head"))
    out_specs = (P("ctx", "head"), P("ctx", "head"), P("ctx", None))
    return jax.shard_map(body, mesh=mesh, in_specs=in_specs, out_specs=out_specs, check_vma=False)
```

time: 171 us -> 62.5 us (0.37)
  the two profiles are of different devices: /device:TPU:7 before, /device:TPU:1 now
where the time goes in v1:
time: 62.5 us; the launch traced here: 62.4 us
  Pallas kernels  55.1 us (88%)
  local copies, waits for them, and re-layouts  6.59 us (11%)
  between operations  0.65 us (1%)
    pallas_call x1, Pallas kernels, body(): pl.pallas_call(kernel, out_shape=(jax.ShapeDtypeStruct((TOK, HEADS * LAT)...  55.1 us
    unnamed x7, local copies, waits for them, and re-layouts  6.59 us

profile of v1, /device:TPU:1, one launch (start us, length us, event | category | flops | bytes accessed | tf_op | source)
XLA Modules:
  0.0 62.4 jit_solution(7407546153277865320)
XLA Ops:
  0.6 55.1 %shard_map.67 = (bf16[192,8192]{1,0:T(8,128)(2,1)}, bf16[192,9216]{1,0:T(8,128)(2,1)}, f32[192,576]{1,0:T(8,128)}) custom-call(bf16[192,9216]{1,0:T(8,128)(2,1)} %q_hbm.1, bf16[192,576]{1,0:T(8,128)(2,1)} %lat_ref.1, s32[1,192]{1,0:T(1,128)} %bitcast.1, bf16[192,8192]{1,0:T(8,128)(2,1)} %do_hbm.1), custom_call_target="tpu_custom_call" | custom-call | tf_op jit(solution)/shard_map/pallas_call | solution.py:364
  55.8 0.0 copy-start
  55.8 4.0 %copy.10 = bf16[192,8192]{1,0:T(8,128)(2,1)} copy(bf16[192,8192]{1,0:T(8,128)(2,1)} %get-tuple-element.6) | data formatting | bytes 6291456
  59.8 0.0 copy-done
  59.8 0.0 copy-start.1
  59.8 1.8 %copy.11 = bf16[192,9216]{1,0:T(8,128)(2,1)} copy(bf16[192,9216]{1,0:T(8,128)(2,1)S(1)} %copy-done) | data formatting | bytes 7077888
  61.6 0.0 copy-done.1
  61.6 0.8 %copy.12 = f32[192,576]{1,0:T(8,128)} copy(f32[192,576]{1,0:T(8,128)S(1)} %copy-done.1) | data formatting | bytes 884736
Async XLA Ops:
  55.8 4.0 %copy-start = (bf16[192,9216]{1,0:T(8,128)(2,1)S(1)}, bf16[192,9216]{1,0:T(8,128)(2,1)}, u32[]{:S(2)}) copy-start(bf16[192,9216]{1,0:T(8,128)(2,1)} %get-tuple-element.7) | copy-start | bytes 10616836
  59.8 1.8 %copy-start.1 = (f32[192,576]{1,0:T(8,128)S(1)}, f32[192,576]{1,0:T(8,128)}, u32[]{:S(2)}) copy-start(f32[192,576]{1,0:T(8,128)} %get-tuple-element.8) | copy-start | bytes 1327108

commit v2 on v0

v2 whole, which is shorter than its diff:
```python
import jax
import jax.numpy as jnp
from jax import lax
from jax.experimental import pallas as pl
from jax.experimental.pallas import tpu as pltpu
from jax.sharding import PartitionSpec as P

TOK = 192
HEADS = 16
PAIRS = HEADS // 2
LAT = 512
WIDTH = 576
PADW = 640
WIN = 512
NCTX = 32
SLICE = 48
PART = 64
SCALE = 192.0 ** -0.5
SCALE2 = SCALE * 1.4426950408889634
bf16 = jnp.bfloat16
f32 = jnp.float32
MESH = pl.DeviceIdType.MESH

GROUPS = ((0, 0, 128, 2, 4, 0), (64, 128, 64, 4, 2, 8))


def dot(a, b):
    return jnp.dot(a, b, preferred_element_type=f32)


def remote(src, dst, send, recv, ctx, head):
    return pltpu.make_async_remote_copy(
        src_ref=src,
        dst_ref=dst,
        send_sem=send,
        recv_sem=recv,
        device_id={"ctx": ctx, "head": head},
        device_id_type=MESH,
    )


def kernel(
    q_hbm, lat_hbm, seg_hbm, do_hbm,
    att, dq, dl,
    q, do, ke, ko, kte, kto, pst, dst, p, ds, bias0, bias1, segs,
    acc, hsum, xs_send, xs_recv, zb_send, zb_recv, ob_send, ob_recv, tb, lat,
    in_sem, send_sem, recv_sem,
):
    here = lax.axis_index("ctx")
    head = lax.axis_index("head")
    y = head // 2
    c = lax.rem(head, 2)
    sib = y * 2 + 1 - c

    def peer(d):
        return lax.rem(y + d, 4) * 2 + c

    has_next = here + 1 + c < NCTX
    has_prev = here >= 1 + c
    sib_prev = here >= 2 - c
    nxt = jnp.minimum(here + 1 + c, NCTX - 1)
    prv = jnp.maximum(here - 1 - c, 0)

    barrier = pltpu.get_barrier_semaphore()

    def greet(ctx, hd):
        pl.semaphore_signal(barrier, inc=1, device_id={"ctx": ctx, "head": hd}, device_id_type=MESH)

    @pl.when(has_next)
    def _():
        for d in range(4):
            greet(nxt, peer(d))

    @pl.when(has_prev)
    def _():
        for d in range(4):
            greet(prv, peer(d))

    greet(here, sib)
    for d in (1, 2, 3):
        greet(here, peer(d))

    get_lat = pltpu.make_async_copy(lat_hbm, lat, in_sem.at[0, PAIRS])
    get_seg = pltpu.make_async_copy(seg_hbm, segs.at[2], in_sem.at[1, PAIRS])
    get_lat.start()
    get_seg.start()

    mine = (1 - c) * TOK
    other = c * TOK

    def rows(base, size):
        return pl.ds(pl.multiple_of(base, 16), size)

    get_seg.wait()
    get_lat.wait()
    ke[2 * TOK :, :] = jnp.concatenate([lat[...], jnp.zeros((TOK, PADW - WIDTH), bf16)], 1)

    @pl.when(jnp.logical_not(has_prev))
    def _():
        ke[rows(mine, TOK), :] = jnp.zeros((TOK, PADW), bf16)
        segs[1 - c] = jnp.full((1, TOK), -1, jnp.int32)

    @pl.when(jnp.logical_not(sib_prev))
    def _():
        ke[rows(other, TOK), :] = jnp.zeros((TOK, PADW), bf16)
        segs[c] = jnp.full((1, TOK), -1, jnp.int32)

    count = 4 + 4 * has_next.astype(jnp.int32) + 4 * has_prev.astype(jnp.int32)
    pl.semaphore_wait(barrier, count)

    def halo(k):
        return remote(
            ke.at[pl.ds(2 * TOK + PART * k, PART)], ke.at[rows(mine + PART * k, PART)],
            send_sem.at[k], recv_sem.at[k], nxt, head,
        )

    def pass_on(k, base):
        w = rows(base + PART * k, PART)
        return remote(ke.at[w], ke.at[w], send_sem.at[4 + k], recv_sem.at[4 + k], here, sib)

    seg_halo = remote(segs.at[2], segs.at[1 - c], send_sem.at[3], recv_sem.at[3], nxt, head)
    seg_pass = remote(segs.at[1 - c], segs.at[1 - c], send_sem.at[7], recv_sem.at[7], here, sib)

    @pl.when(has_next)
    def _():
        seg_halo.start()
        for k in range(3):
            halo(k).start()

    for i in range(PAIRS):
        pltpu.make_async_copy(
            q_hbm.at[:, pl.ds(2 * WIDTH * i, 2 * WIDTH)], q.at[i], in_sem.at[0, i]
        ).start()
        pltpu.make_async_copy(
            do_hbm.at[:, pl.ds(2 * LAT * i, 2 * LAT)], do.at[i], in_sem.at[1, i]
        ).start()

    @pl.when(has_prev)
    def _():
        seg_halo.wait_recv()
        seg_pass.start()
        for k in range(3):
            halo(k).wait_recv()
            pass_on(k, mine).start()

    @pl.when(sib_prev)
    def _():
        seg_pass.wait_recv()

    seg_keys = jnp.broadcast_to(jnp.concatenate([segs[0], segs[1], segs[2]], 1), (TOK, 3 * TOK))
    tok = lax.broadcasted_iota(jnp.int32, (TOK, 3 * TOK), 0) + 2 * TOK
    key = lax.broadcasted_iota(jnp.int32, (TOK, 3 * TOK), 1)
    seg_q = jnp.sum(jnp.where(tok == key, seg_keys, 0), 1, keepdims=True)
    bias = jnp.where((seg_q == seg_keys) & (key <= tok), 0.0, -1e30)
    bias0[...] = bias[:128, :WIN]
    bias1[...] = bias[128:, 64:]

    @pl.when(sib_prev)
    def _():
        for k in range(3):
            pass_on(k, other).wait_recv()

    kev = ke[...]
    ko[...] = jnp.concatenate([jnp.zeros((3 * TOK, PADW - WIDTH), bf16), kev[:, :WIDTH]], 1)
    for g in (0, 1):
        st = GROUPS[g][0]
        kt = kev[st : st + WIN].T
        kte[g] = kt
        kto[g] = jnp.concatenate([jnp.zeros((PADW - WIDTH, WIN), bf16), kt[:WIDTH]], 0)

    def attend(g, i, par):
        _, t0, toks, n, _, first = GROUPS[g]
        bias_ref = (bias0, bias1)[g]
        qs = q[pl.ds(i * n, n), t0 : t0 + toks, par * LAT : par * LAT + PADW].reshape(256, PADW)
        os = do[pl.ds(i * n, n), t0 : t0 + toks, par * LAT : par * LAT + LAT].reshape(256, LAT)
        s = dot(qs, (kte, kto)[par][g])
        dp = dot(os, kte[g, :LAT, :])
        t = ((s * SCALE2).reshape(n, toks, WIN) + bias_ref[...][None]).reshape(256, WIN)
        e = jnp.exp2(t - jnp.max(t, 1, keepdims=True))
        pr = e * (1.0 / jnp.sum(e, 1, keepdims=True))
        delta = jnp.sum(pr * dp, 1, keepdims=True)
        d = (pr * (dp - delta) * SCALE).astype(bf16)
        pr = pr.astype(bf16)
        j = first + i * 2 + par
        p[j] = pr
        ds[j] = d
        cols = pl.ds(pl.multiple_of(g * 1024 + i * 256, 256), 256)
        pst[par, :, cols] = pr.T
        dst[par, :, cols] = d.T

    def wait_pair(i):
        pltpu.make_async_copy(
            q_hbm.at[:, pl.ds(0, 2 * WIDTH)], q.at[i], in_sem.at[0, i]
        ).wait()
        pltpu.make_async_copy(
            do_hbm.at[:, pl.ds(0, 2 * LAT)], do.at[i], in_sem.at[1, i]
        ).wait()

    for i in range(PAIRS):
        wait_pair(i)

    def step0(i, _):
        attend(0, i, 0)
        attend(0, i, 1)
        return 0

    def step1(i, _):
        attend(1, i, 0)
        attend(1, i, 1)
        return 0

    lax.fori_loop(0, 4, step0, 0, unroll=4)
    lax.fori_loop(0, 2, step1, 0, unroll=2)

    def key_grads(lo, hi):
        spans = ((0, lo, min(hi, WIN)), (1, max(lo, 64), hi))
        if hi > WIN:
            spans = spans[::-1]
        for at, (g, a, b) in enumerate(spans):
            st, t0, toks, _, _, _ = GROUPS[g]
            lanes = slice(g * 1024, g * 1024 + toks * PAIRS)
            w = slice(a - st, b - st)
            for par in (0, 1):
                qs = q[:, t0 : t0 + toks, par * LAT : par * LAT + PADW].reshape(toks * PAIRS, PADW)
                r = dot(dst[par, w, lanes], qs)
                acc[par, a:b] = r if at == 0 else acc[par, a:b] + r
            dv = sum(
                dot(
                    pst[par, w, lanes],
                    do[:, t0 : t0 + toks, par * LAT : par * LAT + LAT].reshape(toks * PAIRS, LAT),
                )
                for par in (0, 1)
            )
            acc[0, a:b, :LAT] += dv
        hsum[lo:hi] = acc[0, lo:hi, :WIDTH] + acc[1, lo:hi, PADW - WIDTH :]

    pair_sum = remote(xs_send, xs_recv, send_sem.at[8], recv_sem.at[8], here, sib)

    def send_owners():
        zb_send[...] = (hsum[rows(mine, TOK)] + xs_recv[...].astype(f32)).astype(bf16)

        @pl.when(has_prev)
        def _():
            for d in range(4):
                owner_copy(d).start()

    def owner_copy(d):
        yy = lax.rem(y + d, 4)
        return remote(
            zb_send.at[rows(yy * SLICE, SLICE)], zb_recv.at[y],
            send_sem.at[9 + d], recv_sem.at[9 + y], prv, peer(d),
        )

    def owner_recv(d):
        return remote(
            zb_send.at[pl.ds(0, SLICE)], zb_recv.at[d], send_sem.at[9], recv_sem.at[9 + d], prv, head
        )

    key_grads(0, TOK)

    @pl.when(c == 0)
    def _():
        xs_send[...] = hsum[:TOK].astype(bf16)
        pair_sum.start()

    key_grads(TOK, 2 * TOK)

    @pl.when(c == 1)
    def _():
        xs_send[...] = hsum[TOK : 2 * TOK].astype(bf16)
        pair_sum.start()
        pair_sum.wait_recv()
        send_owners()

    key_grads(2 * TOK, 3 * TOK)
    ob_send[...] = hsum[2 * TOK :].astype(bf16)

    @pl.when(c == 0)
    def _():
        pair_sum.wait_recv()
        send_owners()

    ob = []
    for d in (1, 3, 2):
        cp = remote(
            ob_send.at[rows(lax.rem(y + d, 4) * SLICE, SLICE)], ob_recv.at[d - 1],
            send_sem.at[12 + d], recv_sem.at[12 + d], here, peer(d),
        )
        cp.start()
        ob.append(cp)

    def outputs(g, i):
        st, t0, toks, n, _, first = GROUPS[g]
        j = first + 2 * i
        for par in (0, 1):
            o = dot(p[j + par], ke[st : st + WIN, :LAT]).astype(bf16).reshape(n, toks, LAT)
            for a in range(n):
                col = (2 * (i * n + a) + par) * LAT
                att[t0 : t0 + toks, col : col + LAT] = o[a]
        qe = dot(ds[j], ke[st : st + WIN])
        qo = dot(ds[j + 1], ko[st : st + WIN])
        full = jnp.concatenate(
            [qe[:, :LAT], qe[:, LAT:] + qo[:, : PADW - LAT], qo[:, PADW - LAT :]], 1
        )
        full = full.astype(bf16).reshape(n, toks, 2 * WIDTH)
        for a in range(n):
            col = (i * n + a) * 2 * WIDTH
            dq[t0 : t0 + toks, col : col + 2 * WIDTH] = full[a]

    for i in range(4):
        outputs(0, i)
    for i in range(2):
        outputs(1, i)

    for cp in ob:
        cp.wait_recv()
    part = hsum[pl.ds(pl.multiple_of(2 * TOK + y * SLICE, 8), SLICE)]
    for d in range(3):
        part = part + ob_recv[d].astype(f32)
    hsum[:SLICE] = part

    @pl.when(has_next)
    def _():
        for d in range(4):
            owner_recv(d).wait_recv()
        got = zb_recv[0].astype(f32)
        for d in (1, 2, 3):
            got = got + zb_recv[d].astype(f32)
        hsum[:SLICE] += got

    tb[c, rows(y * SLICE, SLICE)] = hsum[:SLICE].astype(bf16)

    def share(yy, to, k):
        w = (c, rows(yy * SLICE, SLICE))
        return remote(tb.at[w], tb.at[w], send_sem.at[k], recv_sem.at[k], here, to)

    spread = []
    for d in (1, 3, 2):
        cp = share(y, peer(d), 15 + d)
        cp.start()
        spread.append((d, cp))
    last = [share(y, sib, 19)]
    last[0].start()
    for d, cp in spread:
        cp.wait_recv()
        fw = share(lax.rem(y + 4 - d, 4), sib, 19 + d)
        fw.start()
        last.append(fw)
    for cp in last:
        cp.wait_recv()
    dl[...] = tb[0].astype(f32) + tb[1].astype(f32)

    @pl.when(has_next)
    def _():
        seg_halo.wait_send()
        for k in range(3):
            halo(k).wait_send()

    @pl.when(has_prev)
    def _():
        seg_pass.wait_send()
        for k in range(3):
            pass_on(k, mine).wait_send()
        for d in range(4):
            owner_copy(d).wait_send()

    pair_sum.wait_send()
    for cp in ob + [cp for _, cp in spread] + last:
        cp.wait_send()


def write_out(att, dq, dl, att_hbm, dq_hbm, dl_hbm, sem):
    copies = [pltpu.make_async_copy(dl, dl_hbm, sem.at[0])]
    for k in range(4):
        w = pl.ds(k * SLICE, SLICE)
        copies.append(pltpu.make_async_copy(att.at[w], att_hbm.at[w], sem.at[1 + k]))
        copies.append(pltpu.make_async_copy(dq.at[w], dq_hbm.at[w], sem.at[5 + k]))
    for cp in copies:
        cp.start()
    for cp in copies:
        cp.wait()


def pinned(value):
    return pltpu.with_memory_space_constraint(value, pltpu.HBM)


def body(query, latent, segment, d_out):
    hbm = pl.BlockSpec(memory_space=pltpu.HBM)
    vspec = pl.BlockSpec(memory_space=pltpu.VMEM)
    V = pltpu.VMEM
    outs = (((TOK, HEADS * LAT), bf16), ((TOK, HEADS * WIDTH), bf16), ((TOK, WIDTH), f32))
    made = pl.pallas_call(
        kernel,
        out_shape=tuple(V(s, t) for s, t in outs),
        in_specs=[hbm, hbm, hbm, hbm],
        out_specs=(vspec, vspec, vspec),
        scratch_shapes=[
            V((PAIRS, TOK, 2 * WIDTH), bf16),
            V((PAIRS, TOK, 2 * LAT), bf16),
            V((3 * TOK, PADW), bf16),
            V((3 * TOK, PADW), bf16),
            V((2, PADW, WIN), bf16),
            V((2, PADW, WIN), bf16),
            V((2, WIN, 1536), bf16),
            V((2, WIN, 1536), bf16),
            V((12, 256, WIN), bf16),
            V((12, 256, WIN), bf16),
            V((128, WIN), f32),
            V((64, WIN), f32),
            V((3, 1, TOK), jnp.int32),
            V((2, 3 * TOK, PADW), f32),
            V((3 * TOK, WIDTH), f32),
            V((TOK, WIDTH), bf16),
            V((TOK, WIDTH), bf16),
            V((TOK, WIDTH), bf16),
            V((4, SLICE, WIDTH), bf16),
            V((TOK, WIDTH), bf16),
            V((3, SLICE, WIDTH), bf16),
            V((2, TOK, WIDTH), bf16),
            V((TOK, WIDTH), bf16),
            pltpu.SemaphoreType.DMA((2, PAIRS + 1)),
            pltpu.SemaphoreType.DMA((23,)),
            pltpu.SemaphoreType.DMA((23,)),
        ],
        compiler_params=pltpu.CompilerParams(
            collective_id=0, has_side_effects=True, vmem_limit_bytes=44 << 20
        ),
    )(pinned(query), pinned(latent), pinned(segment.reshape(1, TOK)), pinned(d_out))
    return pl.pallas_call(
        write_out,
        out_shape=tuple(jax.ShapeDtypeStruct(s, t) for s, t in outs),
        in_specs=[pl.BlockSpec(memory_space=pl.ANY)] * 3,
        out_specs=(hbm, hbm, hbm),
        scratch_shapes=[pltpu.SemaphoreType.DMA((9,))],
        compiler_params=pltpu.CompilerParams(vmem_limit_bytes=1 << 20),
    )(*made)


def solution(mesh):
    in_specs = (P("ctx", "head"), P("ctx", None), P("ctx"), P("ctx", "head"))
    out_specs = (P("ctx", "head"), P("ctx", "head"), P("ctx", None))
    return jax.shard_map(body, mesh=mesh, in_specs=in_specs, out_specs=out_specs, check_vma=False)
```

time: 171 us -> 50.1 us (0.29); the launches traced: 168 us -> 49.3 us
  waiting for transfers between devices: 57.5 us -> 0 us
  Pallas kernels: 0 us -> 48.5 us
  local copies, waits for them, and re-layouts: 27.9 us -> 0 us
  matrix products: 27.6 us -> 0 us
  starting transfers between devices: 24.7 us -> 0 us
  other arithmetic: 15.8 us -> 0 us
  between operations: 14.3 us -> 0.8 us
    pallas_call x0 -> x2, Pallas kernels: none -> 48.5 us  [the longest x1 45.5 us: body(): pl.pallas_call(kernel, out_shape=tuple((V(s, t) for s, t in outs)), in_sp...]
    psum x1 -> x0, waiting for transfers between devices: 44.3 us -> none  [body(): d_latent = lax.psum(total, 'head')]
    dot_general x6 -> x0, matrix products: 27.6 us -> none  [the longest x1 5.98 us: body(): jnp.einsum('hqk,kd->qhd', d_score, keys, preferred_element_type=jnp.float32)]
    ppermute x6 -> x0, starting transfers between devices: 24.6 us -> none  [shifted(): return lax.ppermute(value, axis, pairs)]
    reshape x3 -> x0, local copies, waits for them, and re-layouts: 16.1 us -> none  [the longest x1 7.05 us: body(): d_query.reshape(rows, heads * width)]
    ppermute x6 -> x0, waiting for transfers between devices: 13.2 us -> none  [shifted(): return lax.ppermute(value, axis, pairs)]
    sub x1 -> x0, other arithmetic: 9.9 us -> none  [body(): expo = jnp.where(allowed[None], jnp.exp(scores - top), 0.0)]
    unnamed x26 -> x0, local copies, waits for them, and re-layouts: 7.48 us -> none
  transfers between devices with their start and end apart: 7 -> 0, of which waited for: 3 -> 0; matrix products, arithmetic and copies ran while one was open for 17% -> 0% of each run, Pallas kernels for 0% -> 0%
where the time goes in v2:
time: 50.1 us; the launch traced here: 49.3 us
  Pallas kernels  48.5 us (97%)
  between operations  0.8 us (2%)
    pallas_call x1, Pallas kernels, body(): pl.pallas_call(kernel, out_shape=tuple((V(s, t) for s, t in outs)), in_sp...  45.5 us
    pallas_call x1, Pallas kernels, body(): pl.pallas_call(write_out, out_shape=tuple((jax.ShapeDtypeStruct(s, t) for...  3.01 us

profile of v2, /device:TPU:7, one launch (start us, length us, event | category | flops | bytes accessed | tf_op | source)
XLA Modules:
  0.0 49.3 jit_solution(5644121096950435898)
XLA Ops:
  0.6 45.5 %shard_map.67 = (bf16[192,8192]{1,0:T(8,128)(2,1)S(1)}, bf16[192,9216]{1,0:T(8,128)(2,1)S(1)}, f32[192,576]{1,0:T(8,128)S(1)}) custom-call(bf16[192,9216]{1,0:T(8,128)(2,1)} %q_hbm.1, bf16[192,576]{1,0:T(8,128)(2,1)} %lat_hbm.1, s32[1,192]{1,0:T(1,128)} %bitcast.1, bf16[192,8192]{1,0:T(8,128)(2,1)} %do_hbm.1), custom_call_target="tpu_custom_call" | custom-call | tf_op jit(solution)/shard_map/pallas_call | solution.py:393
  46.2 3.0 %shard_map.68 = (bf16[192,8192]{1,0:T(8,128)(2,1)}, bf16[192,9216]{1,0:T(8,128)(2,1)}, f32[192,576]{1,0:T(8,128)}) custom-call(bf16[192,8192]{1,0:T(8,128)(2,1)S(1)} %get-tuple-element.6.att, bf16[192,9216]{1,0:T(8,128)(2,1)S(1)} %get-tuple-element.7.dq, f32[192,576]{1,0:T(8,128)S(1)} %get-tuple-element.8.dl), custom_call_target="tpu_custom_call" | custom-call | tf_op jit(solution)/shard_map/pallas_call | solution.py:430

commit v3 on v2

--- a/solution.py
+++ b/solution.py
@@ -14,7 +14,7 @@
 WIN = 512
 NCTX = 32
 SLICE = 48
-PART = 64
+HALF = 96
 SCALE = 192.0 ** -0.5
 SCALE2 = SCALE * 1.4426950408889634
 bf16 = jnp.bfloat16
@@ -43,7 +43,7 @@
     q_hbm, lat_hbm, seg_hbm, do_hbm,
     att, dq, dl,
     q, do, ke, ko, kte, kto, pst, dst, p, ds, bias0, bias1, segs,
-    acc, hsum, xs_send, xs_recv, zb_send, zb_recv, ob_send, ob_recv, tb, lat,
+    acc, hsum, xs_send, xs_recv, zb_send, zb_recv, kb_recv, ob_send, ob_recv, tb, lat,
     in_sem, send_sem, recv_sem,
 ):
     here = lax.axis_index("ctx")
@@ -52,42 +52,53 @@
     c = lax.rem(head, 2)
     sib = y * 2 + 1 - c
 
-    def peer(d):
-        return lax.rem(y + d, 4) * 2 + c
-
-    has_next = here + 1 + c < NCTX
-    has_prev = here >= 1 + c
-    sib_prev = here >= 2 - c
-    nxt = jnp.minimum(here + 1 + c, NCTX - 1)
-    prv = jnp.maximum(here - 1 - c, 0)
+    def at(d, core):
+        return lax.rem(y + d, 4) * 2 + core
+
+    has_next = here + 1 < NCTX
+    has_prev = here >= 1
+    has_two = here >= 2
+    relays = jnp.logical_and(has_next, has_prev)
+    nxt = jnp.minimum(here + 1, NCTX - 1)
+    prv = jnp.maximum(here - 1, 0)
+    first = c == 0
+    second = c == 1
 
     barrier = pltpu.get_barrier_semaphore()
 
     def greet(ctx, hd):
         pl.semaphore_signal(barrier, inc=1, device_id={"ctx": ctx, "head": hd}, device_id_type=MESH)
 
-    @pl.when(has_next)
-    def _():
+    @pl.when(has_prev)
+    def _():
+        greet(prv, head)
+
+    @pl.when(first)
+    def _():
+        @pl.when(has_next)
+        def _():
+            for d in range(4):
+                greet(nxt, at(d, 0))
+
+        @pl.when(relays)
+        def _():
+            greet(nxt, at(0, 1))
+
         for d in range(4):
-            greet(nxt, peer(d))
-
-    @pl.when(has_prev)
+            greet(here, at(d, 1))
+        for d in range(1, 4):
+            greet(here, at(d, 0))
+
+    @pl.when(second)
     def _():
         for d in range(4):
-            greet(prv, peer(d))
-
-    greet(here, sib)
-    for d in (1, 2, 3):
-        greet(here, peer(d))
+            greet(here, at(d, 0))
 
     get_lat = pltpu.make_async_copy(lat_hbm, lat, in_sem.at[0, PAIRS])
     get_seg = pltpu.make_async_copy(seg_hbm, segs.at[2], in_sem.at[1, PAIRS])
     get_lat.start()
     get_seg.start()
 
-    mine = (1 - c) * TOK
-    other = c * TOK
-
     def rows(base, size):
         return pl.ds(pl.multiple_of(base, 16), size)
 
@@ -97,35 +108,46 @@
 
     @pl.when(jnp.logical_not(has_prev))
     def _():
-        ke[rows(mine, TOK), :] = jnp.zeros((TOK, PADW), bf16)
-        segs[1 - c] = jnp.full((1, TOK), -1, jnp.int32)
-
-    @pl.when(jnp.logical_not(sib_prev))
-    def _():
-        ke[rows(other, TOK), :] = jnp.zeros((TOK, PADW), bf16)
-        segs[c] = jnp.full((1, TOK), -1, jnp.int32)
-
-    count = 4 + 4 * has_next.astype(jnp.int32) + 4 * has_prev.astype(jnp.int32)
-    pl.semaphore_wait(barrier, count)
+        ke[TOK : 2 * TOK, :] = jnp.zeros((TOK, PADW), bf16)
+        segs[1] = jnp.full((1, TOK), -1, jnp.int32)
+
+    @pl.when(jnp.logical_not(has_two))
+    def _():
+        ke[:TOK, :] = jnp.zeros((TOK, PADW), bf16)
+        segs[0] = jnp.full((1, TOK), -1, jnp.int32)
+
+    one = has_next.astype(jnp.int32)
+    two = has_prev.astype(jnp.int32)
+    far = has_two.astype(jnp.int32)
+    pl.semaphore_wait(barrier, one + (1 - c) * (4 * two + 7) + c * (far + 4))
 
     def halo(k):
+        w = c * HALF + k * SLICE
         return remote(
-            ke.at[pl.ds(2 * TOK + PART * k, PART)], ke.at[rows(mine + PART * k, PART)],
+            ke.at[rows(2 * TOK + w, SLICE)], ke.at[rows(TOK + w, SLICE)],
             send_sem.at[k], recv_sem.at[k], nxt, head,
         )
 
-    def pass_on(k, base):
-        w = rows(base + PART * k, PART)
-        return remote(ke.at[w], ke.at[w], send_sem.at[4 + k], recv_sem.at[4 + k], here, sib)
-
-    seg_halo = remote(segs.at[2], segs.at[1 - c], send_sem.at[3], recv_sem.at[3], nxt, head)
-    seg_pass = remote(segs.at[1 - c], segs.at[1 - c], send_sem.at[7], recv_sem.at[7], here, sib)
+    def relay(k):
+        w = c * HALF + k * SLICE
+        return remote(
+            ke.at[rows(TOK + w, SLICE)], ke.at[rows(w, SLICE)],
+            send_sem.at[2 + k], recv_sem.at[2 + k], nxt, head,
+        )
+
+    def across(k, blk, core):
+        w = rows(blk * TOK + core * HALF + k * SLICE, SLICE)
+        i = 6 - 2 * blk + k
+        return remote(ke.at[w], ke.at[w], send_sem.at[i], recv_sem.at[i], here, sib)
+
+    seg_halo = remote(segs.at[2], segs.at[1], send_sem.at[8], recv_sem.at[8], nxt, head)
+    seg_relay = remote(segs.at[1], segs.at[0], send_sem.at[9], recv_sem.at[9], nxt, head)
 
     @pl.when(has_next)
     def _():
+        for k in range(2):
+            halo(k).start()
         seg_halo.start()
-        for k in range(3):
-            halo(k).start()
 
     for i in range(PAIRS):
         pltpu.make_async_copy(
@@ -137,15 +159,26 @@
 
     @pl.when(has_prev)
     def _():
+        for k in range(2):
+            halo(k).wait_recv()
+
+            @pl.when(has_next)
+            def _():
+                relay(k).start()
+
+            across(k, 1, c).start()
         seg_halo.wait_recv()
-        seg_pass.start()
-        for k in range(3):
-            halo(k).wait_recv()
-            pass_on(k, mine).start()
-
-    @pl.when(sib_prev)
-    def _():
-        seg_pass.wait_recv()
+
+        @pl.when(has_next)
+        def _():
+            seg_relay.start()
+
+    @pl.when(has_two)
+    def _():
+        for k in range(2):
+            relay(k).wait_recv()
+            across(k, 0, c).start()
+        seg_relay.wait_recv()
 
     seg_keys = jnp.broadcast_to(jnp.concatenate([segs[0], segs[1], segs[2]], 1), (TOK, 3 * TOK))
     tok = lax.broadcasted_iota(jnp.int32, (TOK, 3 * TOK), 0) + 2 * TOK
@@ -155,10 +188,15 @@
     bias0[...] = bias[:128, :WIN]
     bias1[...] = bias[128:, 64:]
 
-    @pl.when(sib_prev)
-    def _():
-        for k in range(3):
-            pass_on(k, other).wait_recv()
+    @pl.when(has_prev)
+    def _():
+        for k in range(2):
+            across(k, 1, 1 - c).wait_recv()
+
+    @pl.when(has_two)
+    def _():
+        for k in range(2):
+            across(k, 0, 1 - c).wait_recv()
 
     kev = ke[...]
     ko[...] = jnp.concatenate([jnp.zeros((3 * TOK, PADW - WIDTH), bf16), kev[:, :WIDTH]], 1)
@@ -234,60 +272,62 @@
             acc[0, a:b, :LAT] += dv
         hsum[lo:hi] = acc[0, lo:hi, :WIDTH] + acc[1, lo:hi, PADW - WIDTH :]
 
-    pair_sum = remote(xs_send, xs_recv, send_sem.at[8], recv_sem.at[8], here, sib)
-
-    def send_owners():
-        zb_send[...] = (hsum[rows(mine, TOK)] + xs_recv[...].astype(f32)).astype(bf16)
-
-        @pl.when(has_prev)
-        def _():
-            for d in range(4):
-                owner_copy(d).start()
-
-    def owner_copy(d):
-        yy = lax.rem(y + d, 4)
+    pair_sum = remote(xs_send, xs_recv, send_sem.at[10], recv_sem.at[10], here, sib)
+
+    def chain(j):
         return remote(
-            zb_send.at[rows(yy * SLICE, SLICE)], zb_recv.at[y],
-            send_sem.at[9 + d], recv_sem.at[9 + y], prv, peer(d),
-        )
-
-    def owner_recv(d):
+            zb_send.at[pl.ds(j * SLICE, SLICE)], kb_recv.at[pl.ds(j * SLICE, SLICE)],
+            send_sem.at[11 + j], recv_sem.at[11 + j], prv, at(0, 0),
+        )
+
+    def deliver(j, slot):
         return remote(
-            zb_send.at[pl.ds(0, SLICE)], zb_recv.at[d], send_sem.at[9], recv_sem.at[9 + d], prv, head
+            zb_send.at[pl.ds(j * SLICE, SLICE)], zb_recv.at[slot],
+            send_sem.at[15 + j], recv_sem.at[15 + slot], prv, j * 2,
+        )
+
+    def own_part(d, core):
+        slot = d - 1 if core == 0 else 3 + d
+        return remote(
+            ob_send.at[rows(lax.rem(y + d, 4) * SLICE, SLICE)], ob_recv.at[slot],
+            send_sem.at[19 + slot], recv_sem.at[19 + slot], here, at(d, 0),
         )
 
     key_grads(0, TOK)
 
-    @pl.when(c == 0)
+    @pl.when(first)
     def _():
         xs_send[...] = hsum[:TOK].astype(bf16)
         pair_sum.start()
 
     key_grads(TOK, 2 * TOK)
 
-    @pl.when(c == 1)
+    @pl.when(second)
     def _():
         xs_send[...] = hsum[TOK : 2 * TOK].astype(bf16)
         pair_sum.start()
         pair_sum.wait_recv()
-        send_owners()
+        zb_send[...] = (hsum[:TOK] + xs_recv[...].astype(f32)).astype(bf16)
+
+        @pl.when(has_two)
+        def _():
+            for j in range(4):
+                chain(j).start()
 
     key_grads(2 * TOK, 3 * TOK)
     ob_send[...] = hsum[2 * TOK :].astype(bf16)
 
-    @pl.when(c == 0)
-    def _():
+    @pl.when(first)
+    def _():
+        for d in (1, 3, 2):
+            own_part(d, 0).start()
         pair_sum.wait_recv()
-        send_owners()
-
-    ob = []
-    for d in (1, 3, 2):
-        cp = remote(
-            ob_send.at[rows(lax.rem(y + d, 4) * SLICE, SLICE)], ob_recv.at[d - 1],
-            send_sem.at[12 + d], recv_sem.at[12 + d], here, peer(d),
-        )
-        cp.start()
-        ob.append(cp)
+        hsum[TOK : 2 * TOK] += xs_recv[...].astype(f32)
+
+    @pl.when(second)
+    def _():
+        for d in (1, 3, 2, 0):
+            own_part(d, 1).start()
 
     def outputs(g, i):
         st, t0, toks, n, _, first = GROUPS[g]
@@ -307,66 +347,117 @@
             col = (i * n + a) * 2 * WIDTH
             dq[t0 : t0 + toks, col : col + 2 * WIDTH] = full[a]
 
-    for i in range(4):
-        outputs(0, i)
-    for i in range(2):
-        outputs(1, i)
-
-    for cp in ob:
-        cp.wait_recv()
-    part = hsum[pl.ds(pl.multiple_of(2 * TOK + y * SLICE, 8), SLICE)]
-    for d in range(3):
-        part = part + ob_recv[d].astype(f32)
-    hsum[:SLICE] = part
+    outputs(0, 0)
+    outputs(0, 1)
+
+    @pl.when(jnp.logical_and(first, has_prev))
+    def _():
+        for j in range(4):
+            w = slice(j * SLICE, (j + 1) * SLICE)
+
+            @pl.when(has_next)
+            def _():
+                chain(j).wait_recv()
+                hsum[TOK + j * SLICE : TOK + (j + 1) * SLICE] += kb_recv[w].astype(f32)
+
+            zb_send[w] = hsum[TOK + j * SLICE : TOK + (j + 1) * SLICE].astype(bf16)
+            deliver(j, y).start()
+
+    outputs(0, 2)
+    outputs(0, 3)
+    outputs(1, 0)
+    outputs(1, 1)
+
+    def share(d, core):
+        w = rows(y * SLICE, SLICE)
+        return remote(
+            tb.at[w], tb.at[w], send_sem.at[26 + 4 * core + d], recv_sem.at[26 + y], here, at(d, core)
+        )
+
+    def shared(d):
+        yy = lax.rem(y + d, 4)
+        w = rows(yy * SLICE, SLICE)
+        return remote(tb.at[w], tb.at[w], send_sem.at[26], recv_sem.at[26 + yy], here, sib)
+
+    @pl.when(first)
+    def _():
+        for d in (1, 2, 3):
+            own_part(d, 0).wait_recv()
+        for d in range(4):
+            own_part(d, 1).wait_recv()
+        part = hsum[pl.ds(pl.multiple_of(2 * TOK + y * SLICE, 8), SLICE)]
+        for k in range(7):
+            part = part + ob_recv[k].astype(f32)
+        hsum[:SLICE] = part
+
+        @pl.when(has_next)
+        def _():
+            for k in range(4):
+                deliver(k, k).wait_recv()
+            got = zb_recv[0].astype(f32)
+            for k in (1, 2, 3):
+                got = got + zb_recv[k].astype(f32)
+            hsum[:SLICE] += got
+
+        tb[rows(y * SLICE, SLICE)] = hsum[:SLICE].astype(bf16)
+        for d, core in ((1, 0), (1, 1), (3, 0), (3, 1), (2, 0), (2, 1), (0, 1)):
+            share(d, core).start()
+        for d in (1, 3, 2):
+            shared(d).wait_recv()
+
+    @pl.when(second)
+    def _():
+        for d in range(4):
+            shared(d).wait_recv()
+
+    dl[...] = tb[...].astype(f32)
 
     @pl.when(has_next)
     def _():
+        for k in range(2):
+            halo(k).wait_send()
+        seg_halo.wait_send()
+
+    @pl.when(has_prev)
+    def _():
+        for k in range(2):
+            across(k, 1, c).wait_send()
+
+    @pl.when(relays)
+    def _():
+        for k in range(2):
+            relay(k).wait_send()
+        seg_relay.wait_send()
+
+    @pl.when(has_two)
+    def _():
+        for k in range(2):
+            across(k, 0, c).wait_send()
+
+    pair_sum.wait_send()
+
+    @pl.when(first)
+    def _():
+        for d in (1, 3, 2):
+            own_part(d, 0).wait_send()
+
+        @pl.when(has_prev)
+        def _():
+            for j in range(4):
+                deliver(j, y).wait_send()
+
+        for d, core in ((1, 0), (1, 1), (3, 0), (3, 1), (2, 0), (2, 1), (0, 1)):
+            share(d, core).wait_send()
+
+    @pl.when(second)
+    def _():
         for d in range(4):
-            owner_recv(d).wait_recv()
-        got = zb_recv[0].astype(f32)
-        for d in (1, 2, 3):
-            got = got + zb_recv[d].astype(f32)
-        hsum[:SLICE] += got
-
-    tb[c, rows(y * SLICE, SLICE)] = hsum[:SLICE].astype(bf16)
-
-    def share(yy, to, k):
-        w = (c, rows(yy * SLICE, SLICE))
-        return remote(tb.at[w], tb.at[w], send_sem.at[k], recv_sem.at[k], here, to)
-
-    spread = []
-    for d in (1, 3, 2):
-        cp = share(y, peer(d), 15 + d)
-        cp.start()
-        spread.append((d, cp))
-    last = [share(y, sib, 19)]
-    last[0].start()
-    for d, cp in spread:
-        cp.wait_recv()
-        fw = share(lax.rem(y + 4 - d, 4), sib, 19 + d)
-        fw.start()
-        last.append(fw)
-    for cp in last:
-        cp.wait_recv()
-    dl[...] = tb[0].astype(f32) + tb[1].astype(f32)
-
-    @pl.when(has_next)
-    def _():
-        seg_halo.wait_send()
-        for k in range(3):
-            halo(k).wait_send()
-
-    @pl.when(has_prev)
-    def _():
-        seg_pass.wait_send()
-        for k in range(3):
-            pass_on(k, mine).wait_send()
-        for d in range(4):
-            owner_copy(d).wait_send()
-
-    pair_sum.wait_send()
-    for cp in ob + [cp for _, cp in spread] + last:
-        cp.wait_send()
+            own_part(d, 1).wait_send()
+
+        @pl.when(has_two)
+        def _():
+            for j in range(4):
+                chain(j).wait_send()
 
 
 def write_out(att, dq, dl, att_hbm, dq_hbm, dl_hbm, sem):
@@ -416,12 +507,13 @@
             V((TOK, WIDTH), bf16),
             V((4, SLICE, WIDTH), bf16),
             V((TOK, WIDTH), bf16),
-            V((3, SLICE, WIDTH), bf16),
-            V((2, TOK, WIDTH), bf16),
+            V((TOK, WIDTH), bf16),
+            V((7, SLICE, WIDTH), bf16),
+            V((TOK, WIDTH), bf16),
             V((TOK, WIDTH), bf16),
             pltpu.SemaphoreType.DMA((2, PAIRS + 1)),
-            pltpu.SemaphoreType.DMA((23,)),
-            pltpu.SemaphoreType.DMA((23,)),
+            pltpu.SemaphoreType.DMA((34,)),
+            pltpu.SemaphoreType.DMA((34,)),
         ],
         compiler_params=pltpu.CompilerParams(
             collective_id=0, has_side_effects=True, vmem_limit_bytes=44 << 20

time: 50.1 us -> 46.9 us (0.936); the launches traced: 49.3 us -> 46.8 us
  Pallas kernels: 48.5 us -> 46 us
    pallas_call x1, Pallas kernels: 45.5 us -> 43 us  [body(): pl.pallas_call(kernel, out_shape=tuple((V(s, t) for s, t in outs)), in_sp...]
where the time goes in v3:
time: 46.9 us; the launch traced here: 46.8 us
  Pallas kernels  46 us (98%)
  between operations  0.8 us (2%)
    pallas_call x1, Pallas kernels, body(): pl.pallas_call(kernel, out_shape=tuple((V(s, t) for s, t in outs)), in_sp...  43 us
    pallas_call x1, Pallas kernels, body(): pl.pallas_call(write_out, out_shape=tuple((jax.ShapeDtypeStruct(s, t) for...  3.01 us

profile of v3, /device:TPU:7, one launch (start us, length us, event | category | flops | bytes accessed | tf_op | source)
XLA Modules:
  0.0 46.8 jit_solution(7938413444547485156)
XLA Ops:
  0.6 43.0 %shard_map.67 = (bf16[192,8192]{1,0:T(8,128)(2,1)S(1)}, bf16[192,9216]{1,0:T(8,128)(2,1)S(1)}, f32[192,576]{1,0:T(8,128)S(1)}) custom-call(bf16[192,9216]{1,0:T(8,128)(2,1)} %q_hbm.1, bf16[192,576]{1,0:T(8,128)(2,1)} %lat_hbm.1, s32[1,192]{1,0:T(1,128)} %bitcast.1, bf16[192,8192]{1,0:T(8,128)(2,1)} %do_hbm.1), custom_call_target="tpu_custom_call" | custom-call | tf_op jit(solution)/shard_map/pallas_call | solution.py:484
  43.7 3.0 %shard_map.68 = (bf16[192,8192]{1,0:T(8,128)(2,1)}, bf16[192,9216]{1,0:T(8,128)(2,1)}, f32[192,576]{1,0:T(8,128)}) custom-call(bf16[192,8192]{1,0:T(8,128)(2,1)S(1)} %get-tuple-element.6.att, bf16[192,9216]{1,0:T(8,128)(2,1)S(1)} %get-tuple-element.7.dq, f32[192,576]{1,0:T(8,128)S(1)} %get-tuple-element.8.dl), custom_call_target="tpu_custom_call" | custom-call | tf_op jit(solution)/shard_map/pallas_call | solution.py:522

commit v4 on v3

--- a/solution.py
+++ b/solution.py
@@ -43,7 +43,7 @@
     q_hbm, lat_hbm, seg_hbm, do_hbm,
     att, dq, dl,
     q, do, ke, ko, kte, kto, pst, dst, p, ds, bias0, bias1, segs,
-    acc, hsum, xs_send, xs_recv, zb_send, zb_recv, kb_recv, ob_send, ob_recv, tb, lat,
+    acc, hsum, xs_send, xs_recv, zb_send, zb_recv, kb_recv, ob_send, ob_recv, tb, lat, t_up, dp_up,
     in_sem, send_sem, recv_sem,
 ):
     here = lax.axis_index("ctx")
@@ -173,53 +173,51 @@
         def _():
             seg_relay.start()
 
-    @pl.when(has_two)
-    def _():
-        for k in range(2):
-            relay(k).wait_recv()
-            across(k, 0, c).start()
-        seg_relay.wait_recv()
-
-    seg_keys = jnp.broadcast_to(jnp.concatenate([segs[0], segs[1], segs[2]], 1), (TOK, 3 * TOK))
     tok = lax.broadcasted_iota(jnp.int32, (TOK, 3 * TOK), 0) + 2 * TOK
     key = lax.broadcasted_iota(jnp.int32, (TOK, 3 * TOK), 1)
-    seg_q = jnp.sum(jnp.where(tok == key, seg_keys, 0), 1, keepdims=True)
-    bias = jnp.where((seg_q == seg_keys) & (key <= tok), 0.0, -1e30)
-    bias0[...] = bias[:128, :WIN]
-    bias1[...] = bias[128:, 64:]
-
-    @pl.when(has_prev)
-    def _():
-        for k in range(2):
-            across(k, 1, 1 - c).wait_recv()
-
-    @pl.when(has_two)
-    def _():
-        for k in range(2):
-            across(k, 0, 1 - c).wait_recv()
-
-    kev = ke[...]
-    ko[...] = jnp.concatenate([jnp.zeros((3 * TOK, PADW - WIDTH), bf16), kev[:, :WIDTH]], 1)
-    for g in (0, 1):
+
+    def mask(seg_row):
+        seg_keys = jnp.broadcast_to(seg_row, (TOK, 3 * TOK))
+        seg_q = jnp.sum(jnp.where(tok == key, seg_keys, 0), 1, keepdims=True)
+        return jnp.where((seg_q == seg_keys) & (key <= tok), 0.0, -1e30)
+
+    def transposed(g, lo, hi):
         st = GROUPS[g][0]
-        kt = kev[st : st + WIN].T
-        kte[g] = kt
-        kto[g] = jnp.concatenate([jnp.zeros((PADW - WIDTH, WIN), bf16), kt[:WIDTH]], 0)
-
-    def attend(g, i, par):
-        _, t0, toks, n, _, first = GROUPS[g]
-        bias_ref = (bias0, bias1)[g]
+        kt = ke[st + lo : st + hi].T
+        kte[g, :, lo:hi] = kt
+        kto[g, :, lo:hi] = jnp.concatenate(
+            [jnp.zeros((PADW - WIDTH, hi - lo), bf16), kt[:WIDTH]], 0
+        )
+
+    def chunk(g, i, par):
+        _, t0, toks, n, _, start = GROUPS[g]
         qs = q[pl.ds(i * n, n), t0 : t0 + toks, par * LAT : par * LAT + PADW].reshape(256, PADW)
         os = do[pl.ds(i * n, n), t0 : t0 + toks, par * LAT : par * LAT + LAT].reshape(256, LAT)
-        s = dot(qs, (kte, kto)[par][g])
-        dp = dot(os, kte[g, :LAT, :])
-        t = ((s * SCALE2).reshape(n, toks, WIN) + bias_ref[...][None]).reshape(256, WIN)
+        return qs, os, start + i * 2 + par
+
+    def scores(g, qs, par, w):
+        _, _, toks, n, _, _ = GROUPS[g]
+        s = dot(qs, (kte, kto)[par][g, :, w])
+        bias = (bias0, bias1)[g][:, w]
+        return ((s * SCALE2).reshape(n, toks, w.stop - w.start) + bias[None]).reshape(256, -1)
+
+    UP = slice(WIN // 2, WIN)
+    LOW = slice(0, WIN // 2)
+
+    def upper(g, i, par):
+        qs, os, j = chunk(g, i, par)
+        t_up[j] = scores(g, qs, par, UP)
+        dp_up[j] = dot(os, kte[g, :LAT, UP])
+
+    def attend(g, i, par):
+        qs, os, j = chunk(g, i, par)
+        t = jnp.concatenate([scores(g, qs, par, LOW), t_up[j]], 1)
+        dp = jnp.concatenate([dot(os, kte[g, :LAT, LOW]), dp_up[j]], 1)
         e = jnp.exp2(t - jnp.max(t, 1, keepdims=True))
         pr = e * (1.0 / jnp.sum(e, 1, keepdims=True))
         delta = jnp.sum(pr * dp, 1, keepdims=True)
         d = (pr * (dp - delta) * SCALE).astype(bf16)
         pr = pr.astype(bf16)
-        j = first + i * 2 + par
         p[j] = pr
         ds[j] = d
         cols = pl.ds(pl.multiple_of(g * 1024 + i * 256, 256), 256)
@@ -234,8 +232,51 @@
             do_hbm.at[:, pl.ds(0, 2 * LAT)], do.at[i], in_sem.at[1, i]
         ).wait()
 
+    @pl.when(has_prev)
+    def _():
+        for k in range(2):
+            across(k, 1, 1 - c).wait_recv()
+
+    near = mask(jnp.concatenate([jnp.full((1, TOK), -1, jnp.int32), segs[1], segs[2]], 1))
+    bias0[:, UP] = near[:128, 256:WIN]
+    bias1[:, UP] = near[128:, 320:]
+    for g in (0, 1):
+        transposed(g, 256, WIN)
     for i in range(PAIRS):
         wait_pair(i)
+
+    def up0(i, _):
+        upper(0, i, 0)
+        upper(0, i, 1)
+        return 0
+
+    def up1(i, _):
+        upper(1, i, 0)
+        upper(1, i, 1)
+        return 0
+
+    lax.fori_loop(0, 4, up0, 0, unroll=4)
+    lax.fori_loop(0, 2, up1, 0, unroll=2)
+
+    @pl.when(has_two)
+    def _():
+        for k in range(2):
+            relay(k).wait_recv()
+            across(k, 0, c).start()
+        seg_relay.wait_recv()
+
+    full_mask = mask(jnp.concatenate([segs[0], segs[1], segs[2]], 1))
+    bias0[:, LOW] = full_mask[:128, :256]
+    bias1[:, LOW] = full_mask[128:, 64:320]
+
+    @pl.when(has_two)
+    def _():
+        for k in range(2):
+            across(k, 0, 1 - c).wait_recv()
+
+    for g in (0, 1):
+        transposed(g, 0, 256)
+    ko[...] = jnp.concatenate([jnp.zeros((3 * TOK, PADW - WIDTH), bf16), ke[:, :WIDTH]], 1)
 
     def step0(i, _):
         attend(0, i, 0)
@@ -347,8 +388,8 @@
             col = (i * n + a) * 2 * WIDTH
             dq[t0 : t0 + toks, col : col + 2 * WIDTH] = full[a]
 
+
     outputs(0, 0)
-    outputs(0, 1)
 
     @pl.when(jnp.logical_and(first, has_prev))
     def _():
@@ -363,10 +404,9 @@
             zb_send[w] = hsum[TOK + j * SLICE : TOK + (j + 1) * SLICE].astype(bf16)
             deliver(j, y).start()
 
+
+    outputs(0, 1)
     outputs(0, 2)
-    outputs(0, 3)
-    outputs(1, 0)
-    outputs(1, 1)
 
     def share(d, core):
         w = rows(y * SLICE, SLICE)
@@ -402,6 +442,13 @@
         tb[rows(y * SLICE, SLICE)] = hsum[:SLICE].astype(bf16)
         for d, core in ((1, 0), (1, 1), (3, 0), (3, 1), (2, 0), (2, 1), (0, 1)):
             share(d, core).start()
+
+    outputs(0, 3)
+    outputs(1, 0)
+    outputs(1, 1)
+
+    @pl.when(first)
+    def _():
         for d in (1, 3, 2):
             shared(d).wait_recv()
 
@@ -511,12 +558,14 @@
             V((7, SLICE, WIDTH), bf16),
             V((TOK, WIDTH), bf16),
             V((TOK, WIDTH), bf16),
+            V((12, 256, WIN // 2), f32),
+            V((12, 256, WIN // 2), f32),
             pltpu.SemaphoreType.DMA((2, PAIRS + 1)),
             pltpu.SemaphoreType.DMA((34,)),
             pltpu.SemaphoreType.DMA((34,)),
         ],
         compiler_params=pltpu.CompilerParams(
-            collective_id=0, has_side_effects=True, vmem_limit_bytes=44 << 20
+            collective_id=0, has_side_effects=True, vmem_limit_bytes=50 << 20
         ),
     )(pinned(query), pinned(latent), pinned(segment.reshape(1, TOK)), pinned(d_out))
     return pl.pallas_call(

time: 46.9 us -> 45 us (0.959)
  Pallas kernels: 46 us -> 44.1 us
    pallas_call x1, Pallas kernels: 43 us -> 41.1 us  [body(): pl.pallas_call(kernel, out_shape=tuple((V(s, t) for s, t in outs)), in_sp...]
where the time goes in v4:
time: 45 us; the launch traced here: 44.9 us
  Pallas kernels  44.1 us (98%)
  between operations  0.8 us (2%)
    pallas_call x1, Pallas kernels, body(): pl.pallas_call(kernel, out_shape=tuple((V(s, t) for s, t in outs)), in_sp...  41.1 us
    pallas_call x1, Pallas kernels, body(): pl.pallas_call(write_out, out_shape=tuple((jax.ShapeDtypeStruct(s, t) for...  3.01 us

profile of v4, /device:TPU:7, one launch (start us, length us, event | category | flops | bytes accessed | tf_op | source)
XLA Modules:
  0.0 44.9 jit_solution(11356427920524929866)
XLA Ops:
  0.6 41.1 %shard_map.67 = (bf16[192,8192]{1,0:T(8,128)(2,1)S(1)}, bf16[192,9216]{1,0:T(8,128)(2,1)S(1)}, f32[192,576]{1,0:T(8,128)S(1)}) custom-call(bf16[192,9216]{1,0:T(8,128)(2,1)} %q_hbm.1, bf16[192,576]{1,0:T(8,128)(2,1)} %lat_hbm.1, s32[1,192]{1,0:T(1,128)} %bitcast.1, bf16[192,8192]{1,0:T(8,128)(2,1)} %do_hbm.1), custom_call_target="tpu_custom_call" | custom-call | tf_op jit(solution)/shard_map/pallas_call | solution.py:531
  41.7 3.0 %shard_map.68 = (bf16[192,8192]{1,0:T(8,128)(2,1)}, bf16[192,9216]{1,0:T(8,128)(2,1)}, f32[192,576]{1,0:T(8,128)}) custom-call(bf16[192,8192]{1,0:T(8,128)(2,1)S(1)} %get-tuple-element.6.att, bf16[192,9216]{1,0:T(8,128)(2,1)S(1)} %get-tuple-element.7.dq, f32[192,576]{1,0:T(8,128)S(1)} %get-tuple-element.8.dl), custom_call_target="tpu_custom_call" | custom-call | tf_op jit(solution)/shard_map/pallas_call | solution.py:571

commit v5 on v4

--- a/solution.py
+++ b/solution.py
@@ -64,6 +64,11 @@
     first = c == 0
     second = c == 1
 
+    get_lat = pltpu.make_async_copy(lat_hbm, lat, in_sem.at[0, PAIRS])
+    get_seg = pltpu.make_async_copy(seg_hbm, segs.at[2], in_sem.at[1, PAIRS])
+    get_lat.start()
+    get_seg.start()
+
     barrier = pltpu.get_barrier_semaphore()
 
     def greet(ctx, hd):
@@ -93,11 +98,6 @@
     def _():
         for d in range(4):
             greet(here, at(d, 0))
-
-    get_lat = pltpu.make_async_copy(lat_hbm, lat, in_sem.at[0, PAIRS])
-    get_seg = pltpu.make_async_copy(seg_hbm, segs.at[2], in_sem.at[1, PAIRS])
-    get_lat.start()
-    get_seg.start()
 
     def rows(base, size):
         return pl.ds(pl.multiple_of(base, 16), size)
@@ -334,19 +334,12 @@
             send_sem.at[19 + slot], recv_sem.at[19 + slot], here, at(d, 0),
         )
 
-    key_grads(0, TOK)
-
-    @pl.when(first)
-    def _():
-        xs_send[...] = hsum[:TOK].astype(bf16)
-        pair_sum.start()
-
-    key_grads(TOK, 2 * TOK)
+    key_grads(0, 2 * TOK)
+    xs_send[...] = hsum[rows(c * TOK, TOK)].astype(bf16)
+    pair_sum.start()
 
     @pl.when(second)
     def _():
-        xs_send[...] = hsum[TOK : 2 * TOK].astype(bf16)
-        pair_sum.start()
         pair_sum.wait_recv()
         zb_send[...] = (hsum[:TOK] + xs_recv[...].astype(f32)).astype(bf16)
 

time: 45 us -> 45 us (level)
  no operation moved by 1% of the time
where the time goes in v5:
time: 45 us; the launch traced here: 44.9 us
  Pallas kernels  44.1 us (98%)
  between operations  0.8 us (2%)
    pallas_call x1, Pallas kernels, body(): pl.pallas_call(kernel, out_shape=tuple((V(s, t) for s, t in outs)), in_sp...  41.1 us
    pallas_call x1, Pallas kernels, body(): pl.pallas_call(write_out, out_shape=tuple((jax.ShapeDtypeStruct(s, t) for...  3.01 us

profile of v5, /device:TPU:7, one launch (start us, length us, event | category | flops | bytes accessed | tf_op | source)
XLA Modules:
  0.0 44.9 jit_solution(10911569055308461961)
XLA Ops:
  0.6 41.1 %shard_map.67 = (bf16[192,8192]{1,0:T(8,128)(2,1)S(1)}, bf16[192,9216]{1,0:T(8,128)(2,1)S(1)}, f32[192,576]{1,0:T(8,128)S(1)}) custom-call(bf16[192,9216]{1,0:T(8,128)(2,1)} %q_hbm.1, bf16[192,576]{1,0:T(8,128)(2,1)} %lat_hbm.1, s32[1,192]{1,0:T(1,128)} %bitcast.1, bf16[192,8192]{1,0:T(8,128)(2,1)} %do_hbm.1), custom_call_target="tpu_custom_call" | custom-call | tf_op jit(solution)/shard_map/pallas_call | solution.py:524
  41.7 3.0 %shard_map.68 = (bf16[192,8192]{1,0:T(8,128)(2,1)}, bf16[192,9216]{1,0:T(8,128)(2,1)}, f32[192,576]{1,0:T(8,128)}) custom-call(bf16[192,8192]{1,0:T(8,128)(2,1)S(1)} %get-tuple-element.6.att, bf16[192,9216]{1,0:T(8,128)(2,1)S(1)} %get-tuple-element.7.dq, f32[192,576]{1,0:T(8,128)S(1)} %get-tuple-element.8.dl), custom_call_target="tpu_custom_call" | custom-call | tf_op jit(solution)/shard_map/pallas_call | solution.py:564
